TPU v7x, 128 devices: a whole 4x4x4 slice. The times are simulated.
128 devices in a mesh: dp: 2 (over x_lo), tm: 16 (over z, x_hi, core), elec: 4 (over y).
Axes of the slice: x: 4 (x_hi: 2, x_lo: 2; x = x_hi * 2 + x_lo), y: 4, z: 4, core: 2. Of those that a mesh axis runs over, the one named last changes fastest.
Arguments:
- inputs: bfloat16 [2, 16, 6144, 512], P('dp', 'elec', 'tm'), may hold values from -12 to 12
- cotangent: bfloat16 [2, 16, 6144, 512], P('dp', 'elec', 'tm'), may hold values from -24 to 24
- w_query: bfloat16 [512, 512], replicated, may hold values from -0.375 to 0.375
- w_key: bfloat16 [512, 512], replicated, may hold values from -0.375 to 0.375
- w_value: bfloat16 [512, 512], replicated, may hold values from -0.25 to 0.25
- w_out: bfloat16 [512, 512], replicated, may hold values from -0.25 to 0.25
Outputs:
- grad_inputs: bfloat16 [2, 16, 6144, 512], P('dp', 'elec', 'tm')
- grad_w_query: float32 [512, 512], replicated
- grad_w_key: float32 [512, 512], replicated
- grad_w_value: float32 [512, 512], replicated
- grad_w_out: float32 [512, 512], replicated
All inputs are finite; a program needn't handle non-finite values.
Results may differ from a plain program's by a relative error of at most 0.012.
The roundings to bfloat16 on the way count: a program that leaves them out, or rounds other values in their place, can miss the bound.
Values may be sent and summed in bfloat16 or wider, within the bound.
A program may use at most 192 MiB of HBM per device.

v0:
```python
import functools
import math

import jax
import jax.numpy as jnp
from jax import lax
from jax.experimental import pallas as pl
from jax.experimental.pallas import tpu as pltpu
from jax.sharding import PartitionSpec as P

BF16 = jnp.bfloat16
F32 = jnp.float32
WIN = 128
HALF = 256
HEAD = 64
HEADS = 4
NEG = -1e30
SCALE = 0.125
VMEM_LIMIT = 56 * 1024 * 1024
MESH = pl.DeviceIdType.MESH

NN = (((1,), (0,)), ((), ()))
NT = (((1,), (1,)), ((), ()))
TN = (((0,), (0,)), ((), ()))


def mm(left, right, dims):
    return lax.dot_general(left, right, dims, preferred_element_type=F32)


def stack_heads(rows):
    head = lax.broadcasted_iota(jnp.int32, (1, HALF), 1) // HEAD
    return jnp.concatenate(
        [rows * (head == h).astype(F32).astype(BF16) for h in range(HEADS)], axis=0
    )


def pick_heads(rows):
    count = rows.shape[0] // HEADS
    head = lax.broadcasted_iota(jnp.int32, (count, HALF), 1) // HEAD
    out = rows[:count]
    for h in range(1, HEADS):
        out = jnp.where(head == h, rows[h * count : (h + 1) * count], out)
    return out


def soft(scores, grad_probs):
    peak = jnp.max(scores, axis=0, keepdims=True)
    ex = jnp.exp(scores - peak)
    probs = ex / jnp.sum(ex, axis=0, keepdims=True)
    delta = jnp.sum(probs * grad_probs, axis=0, keepdims=True)
    return probs, probs * (grad_probs - delta)


def temporal_block(q, ga, k, v, bias):
    qs, gs = stack_heads(q), stack_heads(ga)
    st = mm(k, qs, NT)
    gt = mm(v, gs, NT)
    shape = (WIN, HEADS * WIN)
    older = lax.broadcasted_iota(jnp.int32, shape, 0) > lax.rem(
        lax.broadcasted_iota(jnp.int32, shape, 1), WIN
    )
    probs, grad = soft(
        jnp.where(older, st[:WIN] + bias, st[WIN:]), jnp.where(older, gt[:WIN], gt[WIN:])
    )

    def spread(t):
        return jnp.concatenate(
            [jnp.where(older, t, 0.0).astype(BF16), jnp.where(older, 0.0, t).astype(BF16)], axis=0
        )

    pt, dt = spread(probs), spread(grad)
    att = pick_heads(mm(pt, v, TN))
    dq = pick_heads(mm(dt, k, TN)) * SCALE
    return att, dq, mm(dt, qs, NN), mm(pt, gs, NN)


def spatial_block(q, ga, k, v):
    qs, gs = stack_heads(q), stack_heads(ga)
    shape = (WIN, HEADS * WIN)
    same = lax.rem(lax.broadcasted_iota(jnp.int32, shape, 0), 8) == lax.rem(
        lax.broadcasted_iota(jnp.int32, shape, 1), 8
    )
    probs, grad = soft(jnp.where(same, mm(k, qs, NT), NEG), mm(v, gs, NT))
    pt, dt = probs.astype(BF16), grad.astype(BF16)
    att = pick_heads(mm(pt, v, TN))
    dq = pick_heads(mm(dt, k, TN)) * SCALE
    return att, dq, mm(dt, qs, NN), mm(pt, gs, NN)


def join_weights(w_refs, first, w_all):
    for i, w in enumerate(w_refs):
        w_all[:, i * HALF : (i + 1) * HALF] = w[:, first : first + HALF]


def temporal_kernel(
    x, halo, cot, wq, wk, wv, wo, att_o, dq_o, dk_o, dv_o, back_o, w_all, q_s, k_s, v_s, g_s, dk_s, dv_s
):
    elecs, patches, width = x.shape
    join_weights((wq, wk, wv), HALF, w_all)
    bias0 = jnp.where(lax.axis_index("tm") == 0, NEG, 0.0).astype(F32)

    def electrode(e, carry):
        xe = x[e]
        q_s[...] = (mm(xe, w_all[:, :HALF], NN) * SCALE).astype(BF16)
        ext = jnp.concatenate([halo[e], xe], axis=0)
        k_s[...] = mm(ext, w_all[:, HALF : 2 * HALF], NN).astype(BF16)
        v_s[...] = mm(ext, w_all[:, 2 * HALF :], NN).astype(BF16)
        g_s[...] = mm(cot[e], wo[HALF:, :], NT).astype(BF16)
        dk_s[...] = jnp.zeros_like(dk_s)
        dv_s[...] = jnp.zeros_like(dv_s)
        for c in range(patches // WIN):
            rows = slice(c * WIN, (c + 1) * WIN)
            keys = slice(c * WIN, (c + 2) * WIN)
            att, dq, dk, dv = temporal_block(
                q_s[rows], g_s[rows], k_s[keys], v_s[keys], bias0 if c == 0 else 0.0
            )
            att_o[e, rows] = att.astype(BF16)
            dq_o[e, rows] = dq.astype(BF16)
            dk_s[keys] += dk
            dv_s[keys] += dv
        back_o[0, e] = dk_s[:WIN].astype(BF16)
        back_o[1, e] = dv_s[:WIN].astype(BF16)
        dk_o[e] = dk_s[WIN:]
        dv_o[e] = dv_s[WIN:]
        return carry

    lax.fori_loop(0, elecs, electrode, 0)


def weight_rows(acc_in, acc_out, w_o):
    for i in range(3):
        w_o[i * 512 : (i + 1) * 512] = acc_in[:, i * HALF : (i + 1) * HALF].astype(BF16)
    w_o[1536:1792] = acc_out[:, :HALF].astype(BF16)
    w_o[1792:2048] = acc_out[:, HALF:].astype(BF16)


def temporal_end_kernel(
    x, cot, att, dq, dk, dv, back, wq, wk, wv, dx_o, w_o, w_all, acc_in, acc_out
):
    elecs, patches, width = x.shape
    join_weights((wq, wk, wv), HALF, w_all)
    acc_in[...] = jnp.zeros_like(acc_in)
    acc_out[...] = jnp.zeros_like(acc_out)

    def electrode(e, carry):
        def full(own, side):
            tail = own[e, patches - WIN :] + back[side, e].astype(F32)
            return jnp.concatenate(
                [own[e, : patches - WIN].astype(BF16), tail.astype(BF16)], axis=0
            )

        grads = jnp.concatenate([dq[e], full(dk, 0), full(dv, 1)], axis=1)
        dx_o[e] = mm(grads, w_all[...], NT)
        acc_in[...] += mm(x[e], grads, TN)
        acc_out[...] += mm(att[e], cot[e], TN)
        return carry

    lax.fori_loop(0, elecs, electrode, 0)
    weight_rows(acc_in, acc_out, w_o)


def spatial_kernel(*refs):
    xs, cots = refs[0:4], refs[4:8]
    wq, wk, wv, wo = refs[8:12]
    dxs, w_o = refs[12:16], refs[16]
    w_all, q_s, k_s, v_s, g_s, acc_in, acc_out = refs[17:]
    elecs, patches, width = xs[0].shape
    rows = elecs * patches
    join_weights((wq, wk, wv), 0, w_all)

    def split(t):
        return t.reshape(elecs, patches, HALF)

    for i in range(4):
        part = slice(i * elecs, (i + 1) * elecs)
        xi = xs[i][...].reshape(rows, width)
        q_s[part] = split(mm(xi, w_all[:, :HALF], NN) * SCALE)
        k_s[part] = split(mm(xi, w_all[:, HALF : 2 * HALF], NN))
        v_s[part] = split(mm(xi, w_all[:, 2 * HALF :], NN))
        g_s[part] = split(mm(cots[i][...].reshape(rows, width), wo[:HALF, :], NT))

    def block(g, carry):
        at = pl.ds(pl.multiple_of(g * 8, 8), 8)

        def load(ref):
            return ref[:, at, :].reshape(WIN, HALF).astype(BF16)

        def store(ref, value):
            ref[:, at, :] = value.reshape(4 * elecs, 8, HALF)

        att, dq, dk, dv = spatial_block(load(q_s), load(g_s), load(k_s), load(v_s))
        store(g_s, att)
        store(q_s, dq)
        store(k_s, dk)
        store(v_s, dv)
        return carry

    lax.fori_loop(0, patches // 8, block, 0)

    for i in range(4):
        part = slice(i * elecs, (i + 1) * elecs)
        xi = xs[i][...].reshape(rows, width)
        grads = jnp.concatenate(
            [ref[part].astype(BF16).reshape(rows, HALF) for ref in (q_s, k_s, v_s)], axis=1
        )
        dxs[i][...] = mm(grads, w_all[...], NT).astype(BF16).reshape(elecs, patches, width)
        add_in = mm(xi, grads, TN)
        add_out = mm(
            g_s[part].astype(BF16).reshape(rows, HALF), cots[i][...].reshape(rows, width), TN
        )
        if i == 0:
            acc_in[...] = add_in
            acc_out[...] = add_out
        else:
            acc_in[...] += add_in
            acc_out[...] += add_out
    weight_rows(acc_in, acc_out, w_o)


def final_kernel(dx, p0, p1, p2, p3, out):
    me = lax.axis_index("elec")
    patches = p0.shape[1]
    for d, piece in enumerate((p0, p1, p2, p3)):
        at = pl.ds(pl.multiple_of(lax.rem(me + d, 4) * patches, 16), patches)
        out[:, at, :] = (dx[:, at, :] + piece[...].astype(F32)).astype(BF16)


def coordinates():
    dp, tm, y = lax.axis_index("dp"), lax.axis_index("tm"), lax.axis_index("elec")
    z, rest = lax.div(tm, 4), lax.rem(tm, 4)
    x = lax.div(rest, 2) * 2 + dp
    return x, y, z, lax.rem(rest, 2)


def device_at(x, y, z, core):
    return {"dp": lax.rem(x, 2), "tm": z * 4 + lax.div(x, 2) * 2 + core, "elec": y}


def sum_kernel(wt, ws, out, recv_c, part_c, recv_a, part_a, recv_b, part_b, recv_e, send_sem, recv_sem):
    x, y, z, core = coordinates()
    other_core = device_at(x, y, z, 1 - core)

    def peer(axis, d):
        if axis == "x":
            return device_at(lax.rem(x + d, 4), y, z, core)
        if axis == "y":
            return device_at(x, lax.rem(y + d, 4), z, core)
        return device_at(x, y, lax.rem(z + d, 4), core)

    where = {"x": x, "y": y, "z": z}
    barrier = pltpu.get_barrier_semaphore()
    pl.semaphore_signal(barrier, inc=1, device_id=other_core, device_id_type=MESH)
    for axis in "xyz":
        for d in range(1, 4):
            pl.semaphore_signal(barrier, inc=1, device_id=peer(axis, d), device_id_type=MESH)
    pl.semaphore_wait(barrier, 10)

    orders = ("xzy", "zxy")
    sources = (wt, ws)
    started = []

    def start(p, n, src, dst, device):
        copy = pltpu.make_async_remote_copy(
            src_ref=src,
            dst_ref=dst,
            send_sem=send_sem.at[p, n],
            recv_sem=recv_sem.at[p, n],
            device_id=device,
            device_id_type=MESH,
        )
        copy.start()
        started.append(copy)
        return copy

    def block(first, size):
        return pl.ds(pl.multiple_of(first, 16), size)

    waiting = []
    for p in range(2):
        waiting.append([start(p, 0, sources[p].at[block((1 - core) * 1024, 1024)], recv_c.at[p], other_core)])
    base = [core * 1024, core * 1024]
    source, size = None, 1024
    stages = ((recv_a, part_c), (recv_b, part_a), (recv_e, part_b))
    for stage in range(3):
        size = size // 4
        landing, held = stages[stage]
        for p in range(2):
            for copy in waiting[p]:
                copy.wait_recv()
            if stage == 0:
                total = sources[p][block(core * 1024, 1024)].astype(F32) + recv_c[p].astype(F32)
            else:
                arrived, before = stages[stage - 1]
                spot = where[orders[p][stage - 1]]
                total = before[p, block(spot * size * 4, size * 4)].astype(F32)
                for d in range(3):
                    total = total + arrived[p, d].astype(F32)
            held[p] = total.astype(BF16)
            axis = orders[p][stage]
            waiting[p] = []
            for d in range(1, 4):
                to = lax.rem(where[axis] + d, 4)
                waiting[p].append(
                    start(
                        p,
                        1 + stage * 3 + d - 1,
                        held.at[p, block(to * size, size)],
                        landing.at[p, d - 1],
                        peer(axis, d),
                    )
                )
            base[p] = base[p] + where[axis] * size
    for p in range(2):
        for copy in waiting[p]:
            copy.wait_recv()
        total = part_b[p, block(where["y"] * 16, 16)].astype(F32)
        for d in range(3):
            total = total + recv_e[p, d].astype(F32)
        out[p, block(base[p], 16)] = total.astype(BF16)
        waiting[p] = []
    for stage in (2, 1, 0):
        for p in range(2):
            for copy in waiting[p]:
                copy.wait_recv()
            axis = orders[p][stage]
            rows = block(base[p], size)
            waiting[p] = [
                start(p, 10 + stage * 3 + d - 1, out.at[p, rows], out.at[p, rows], peer(axis, d))
                for d in range(1, 4)
            ]
            base[p] = base[p] - where[axis] * size
        size = size * 4
    for p in range(2):
        for copy in waiting[p]:
            copy.wait_recv()
        rows = block(core * 1024, 1024)
        waiting[p] = [start(p, 19, out.at[p, rows], out.at[p, rows], other_core)]
    for p in range(2):
        for copy in waiting[p]:
            copy.wait_recv()
    for copy in started:
        copy.wait_send()


def call(kernel, outs, scratch, flops, **more):
    params = {"vmem_limit_bytes": VMEM_LIMIT, **more}

    def run(*args):
        return pl.pallas_call(
            kernel,
            out_shape=outs,
            in_specs=[pl.BlockSpec(memory_space=pltpu.VMEM)] * len(args),
            out_specs=jax.tree.map(lambda _: pl.BlockSpec(memory_space=pltpu.VMEM), outs),
            scratch_shapes=scratch,
            compiler_params=pltpu.CompilerParams(**params),
            cost_estimate=pl.CostEstimate(
                flops=flops, bytes_accessed=8 * 1024 * 1024, transcendentals=1024 * 1024
            ),
        )(*args)

    return run


def sds(shape, dtype):
    return jax.ShapeDtypeStruct(shape, dtype)


def rotate(block, axis, distance):
    count = lax.axis_size(axis)
    return lax.ppermute(block, axis, [(i, (i + distance) % count) for i in range(count)])


def shifted(block, axis, distance):
    devices = range(lax.axis_size(axis))
    return lax.ppermute(
        block, axis, [(i - distance, i) for i in devices if i - distance in devices]
    )


def shards(inputs, cotangent, w_query, w_key, w_value, w_out):
    _, elecs, patches, width = inputs.shape
    x, cot = inputs[0], cotangent[0]
    quarter = patches // 4
    me = lax.axis_index("elec")
    halo = shifted(x[:, patches - WIN :], "tm", 1)

    def piece(t, d):
        return lax.dynamic_slice_in_dim(t, lax.rem(me + d, 4) * quarter, quarter, 1)

    xs = [piece(x, 0)] + [rotate(piece(x, d), "elec", d) for d in (2, 1, 3)]
    cots = [piece(cot, 0)] + [rotate(piece(cot, d), "elec", d) for d in (2, 1, 3)]

    vm = pltpu.VMEM
    att, dq, dk, dv, back = call(
        temporal_kernel,
        (
            sds((elecs, patches, HALF), BF16),
            sds((elecs, patches, HALF), BF16),
            sds((elecs, patches, HALF), F32),
            sds((elecs, patches, HALF), F32),
            sds((2, elecs, WIN, HALF), BF16),
        ),
        [
            vm((width, 3 * HALF), BF16),
            vm((patches, HALF), BF16),
            vm((patches + WIN, HALF), BF16),
            vm((patches + WIN, HALF), BF16),
            vm((patches, HALF), BF16),
            vm((patches + WIN, HALF), F32),
            vm((patches + WIN, HALF), F32),
        ],
        10**10,
    )(x, halo, cot, w_query, w_key, w_value, w_out)
    back = shifted(back, "tm", -1)
    dx_time, wt = call(
        temporal_end_kernel,
        (sds((elecs, patches, width), F32), sds((2048, HALF), BF16)),
        [vm((width, 3 * HALF), BF16), vm((width, 3 * HALF), F32), vm((HALF, width), F32)],
        5 * 10**9,
    )(x, cot, att, dq, dk, dv, back, w_query, w_key, w_value)
    *dxs, ws = call(
        spatial_kernel,
        tuple([sds((elecs, quarter, width), BF16)] * 4) + (sds((2048, HALF), BF16),),
        [vm((width, 3 * HALF), BF16)]
        + [vm((4 * elecs, quarter, HALF), F32)] * 4
        + [vm((width, 3 * HALF), F32), vm((HALF, width), F32)],
        10**10,
    )(*xs, *cots, w_query, w_key, w_value, w_out)
    by_back = {0: dxs[0], 2: dxs[1], 1: dxs[2], 3: dxs[3]}
    pieces = [by_back[0]] + [rotate(by_back[d], "elec", -d) for d in (1, 2, 3)]
    grad_inputs = call(final_kernel, sds((elecs, patches, width), BF16), [], 10**7)(
        dx_time, *pieces
    )
    dma = pltpu.SemaphoreType.DMA
    sums = call(
        sum_kernel,
        sds((2, 2048, HALF), BF16),
        [
            vm((2, 1024, HALF), BF16),
            vm((2, 1024, HALF), BF16),
            vm((2, 3, 256, HALF), BF16),
            vm((2, 256, HALF), BF16),
            vm((2, 3, 64, HALF), BF16),
            vm((2, 64, HALF), BF16),
            vm((2, 3, 16, HALF), BF16),
            dma((2, 20)),
            dma((2, 20)),
        ],
        10**9,
        collective_id=0,
        has_side_effects=True,
    )(wt, ws)
    sums = sums.astype(F32) * (1.0 / math.sqrt(196608))
    time, space = sums[0], sums[1]
    grads = [
        jnp.concatenate([space[i : i + 512], time[i : i + 512]], axis=1) for i in (0, 512, 1024)
    ]
    grad_out = jnp.concatenate(
        [jnp.concatenate([t[1536:1792], t[1792:2048]], axis=1) for t in (space, time)], axis=0
    )
    return (grad_inputs[None], grads[0], grads[1], grads[2], grad_out)


def solution(mesh):
    return jax.shard_map(
        shards,
        mesh=mesh,
        in_specs=(P("dp", "elec", "tm", None), P("dp", "elec", "tm", None), P(), P(), P(), P()),
        out_specs=(P("dp", "elec", "tm", None), P(), P(), P(), P()),
        check_vma=False,
    )
```

profile of v0, /device:TPU:1, one launch (start us, length us, event | category | flops | bytes accessed | tf_op | source)
XLA Modules:
  0.0 132.6 jit_solution(2450960369338308188)
XLA Ops:
  0.6 0.0 copy-start
  0.6 1.2 slice.96
  1.8 6.0 %collective-permute-start = (bf16[4,128,512]{2,1,0:T(8,128)(2,1)S(1)}, bf16[4,128,512]{2,1,0:T(8,128)(2,1)S(1)}, u32[]{:S(2)}, u32[]{:S(2)}) collective-permute-start(bf16[4,128,512]{2,1,0:T(8,128)(2,1)S(1)} %slice.96), channel_id=1, source_target_pairs={{0,4},{4,8},{8,12},{12,16},{16,20},{20,24},{24,28},{28,32},{32,36}... | collective-permute-start | bytes 1572872 | tf_op jit(solution)/shard_map/ppermute | solution.py:376
  7.9 2.3 %dynamic-slice_bitcast_fusion.4 = (bf16[4,96,512]{2,1,0:T(8,128)(2,1)S(1)}, bf16[4,96,512]{2,1,0:T(8,128)(2,1)S(1)}, bf16[4,96,512]{2,1,0:T(8,128)(2,1)}, bf16[4,96,512]{2,1,0:T(8,128)(2,1)S(1)}) fusion(bf16[1,4,384,512]{3,2,1,0:T(8,128)(2,1)} %param.6, s32[]{:T(128)S(6)} %select_n.19, s32[]{:T(128)S(6)} %select_n.17, s32[]{:T(128)S(6)} %select_n.16, ...), kind=kLoop, calls=%fused_computation.15 | loop fusion | bytes 3145744 | tf_op jit(solution)/shard_map/dynamic_slice | solution.py:389
  10.2 2.9 %collective-permute-start.2 = (bf16[4,96,512]{2,1,0:T(8,128)(2,1)S(1)}, bf16[4,96,512]{2,1,0:T(8,128)(2,1)S(1)}, u32[]{:S(2)}, u32[]{:S(2)}) collective-permute-start(bf16[4,96,512]{2,1,0:T(8,128)(2,1)S(1)} %get-tuple-element.44), channel_id=1, source_target_pairs={{0,2},{1,3},{2,0},{3,1},{4,6},{5,7},{6,4},{7,5},{8,10},{9,11},{10,... | collective-permute-start | bytes 1179656 | tf_op jit(solution)/shard_map/ppermute | solution.py:371
  13.1 0.4 collective-permute-start.3
  13.5 2.3 %collective-permute-start.4 = (bf16[4,96,512]{2,1,0:T(8,128)(2,1)S(1)}, bf16[4,96,512]{2,1,0:T(8,128)(2,1)S(1)}, u32[]{:S(2)}, u32[]{:S(2)}) collective-permute-start(bf16[4,96,512]{2,1,0:T(8,128)(2,1)S(1)} %get-tuple-element.43), channel_id=1, source_target_pairs={{0,3},{1,0},{2,1},{3,2},{4,7},{5,4},{6,5},{7,6},{8,11},{9,8},{10,9... | collective-permute-start | bytes 1179656 | tf_op jit(solution)/shard_map/ppermute | solution.py:371
  15.8 0.0 copy-done
  15.8 0.9 dynamic-slice_bitcast_fusion
  16.7 0.0 collective-permute-start.5
  16.7 5.9 %collective-permute-done.2.refs_1_ = bf16[4,96,512]{2,1,0:T(8,128)(2,1)S(1)} collective-permute-done((bf16[4,96,512]{2,1,0:T(8,128)(2,1)S(1)}, bf16[4,96,512]{2,1,0:T(8,128)(2,1)S(1)}, u32[]{:S(2)}, u32[]{:S(2)}) %collective-permute-start.2) | collective-permute-done | bytes 393248 | tf_op jit(solution)/shard_map/ppermute | solution.py:371
  22.6 1.3 collective-permute-start.6
  23.9 0.0 collective-permute-done.halo
  23.9 1.5 %collective-permute-start.7 = (bf16[4,96,512]{2,1,0:T(8,128)(2,1)S(1)}, bf16[4,96,512]{2,1,0:T(8,128)(2,1)S(1)}, u32[]{:S(2)}, u32[]{:S(2)}) collective-permute-start(bf16[4,96,512]{2,1,0:T(8,128)(2,1)S(1)} %get-tuple-element.39), channel_id=1, source_target_pairs={{0,3},{1,0},{2,1},{3,2},{4,7},{5,4},{6,5},{7,6},{8,11},{9,8},{10,9... | collective-permute-start | bytes 1179656 | tf_op jit(solution)/shard_map/ppermute | solution.py:371
  25.5 0.0 copy-done.4
  25.5 15.1 %shard_map.101 = (bf16[4,384,256]{2,1,0:T(8,128)(2,1)}, bf16[4,384,256]{2,1,0:T(8,128)(2,1)}, f32[4,384,256]{2,1,0:T(8,128)}, f32[4,384,256]{2,1,0:T(8,128)}, bf16[2,4,128,256]{3,2,1,0:T(8,128)(2,1)}) custom-call(bf16[4,384,512]{2,1,0:T(8,128)(2,1)} %bitcast.40, bf16[4,128,512]{2,1,0:T(8,128)(2,1)} %copy-done.4, bf16[4,384,512]{2,1,0:T(8,128)(2,1)} %bitcast.42, ...), custom_call_target="tpu_custom_call" | custom-call | flops 10000000000 | bytes 8388608 | tf_op jit(solution)/shard_map/pallas_call | solution.py:350
  40.6 0.0 copy-done.6
  40.6 0.0 collective-permute-done.3.refs_2_
  40.6 0.0 copy-start.7
  40.6 1.9 %collective-permute-start.1 = (bf16[2,4,128,256]{3,2,1,0:T(8,128)(2,1)}, bf16[2,4,128,256]{3,2,1,0:T(8,128)(2,1)S(1)}, u32[]{:S(2)}, u32[]{:S(2)}) collective-permute-start(bf16[2,4,128,256]{3,2,1,0:T(8,128)(2,1)} %get-tuple-element.21), channel_id=1, source_target_pairs={{4,0},{8,4},{12,8},{16,12},{20,16},{24,20},{28,24},{32,28},{36,32}... | collective-permute-start | bytes 1572872 | tf_op jit(solution)/shard_map/ppermute | solution.py:376
  42.5 0.0 collective-permute-done.4.refs_3_
  42.5 0.0 copy-start.8
  42.5 0.0 collective-permute-done.5.refs_5_
  42.6 2.8 %collective-permute-done.6.refs_6_ = bf16[4,96,512]{2,1,0:T(8,128)(2,1)S(1)} collective-permute-done((bf16[4,96,512]{2,1,0:T(8,128)(2,1)S(1)}, bf16[4,96,512]{2,1,0:T(8,128)(2,1)S(1)}, u32[]{:S(2)}, u32[]{:S(2)}) %collective-permute-start.6) | collective-permute-done | bytes 393248 | tf_op jit(solution)/shard_map/ppermute | solution.py:371
  45.4 0.6 collective-permute-done.7.refs_7_
  45.9 0.2 copy-done.10
  46.1 0.6 copy-done.11
  46.7 17.4 %shard_map.103 = (bf16[4,96,512]{2,1,0:T(8,128)(2,1)}, bf16[4,96,512]{2,1,0:T(8,128)(2,1)}, bf16[4,96,512]{2,1,0:T(8,128)(2,1)}, bf16[4,96,512]{2,1,0:T(8,128)(2,1)}, bf16[2048,256]{1,0:T(8,128)(2,1)}) custom-call(bf16[4,96,512]{2,1,0:T(8,128)(2,1)} %get-tuple-element.45.refs_0_, bf16[4,96,512]{2,1,0:T(8,128)(2,1)} %copy-done.6, ...), custom_call_target="tpu_custom_call" | custom-call | flops 10000000000 | bytes 8388608 | tf_op jit(solution)/shard_map/pallas_call | solution.py:350
  64.1 2.5 %collective-permute-start.8 = (bf16[4,96,512]{2,1,0:T(8,128)(2,1)}, bf16[4,96,512]{2,1,0:T(8,128)(2,1)S(1)}, u32[]{:S(2)}, u32[]{:S(2)}) collective-permute-start(bf16[4,96,512]{2,1,0:T(8,128)(2,1)} %get-tuple-element.24), channel_id=1, source_target_pairs={{0,3},{1,0},{2,1},{3,2},{4,7},{5,4},{6,5},{7,6},{8,11},{9,8},{10,9... | collective-permute-start | bytes 1179656 | tf_op jit(solution)/shard_map/ppermute | solution.py:371
  66.6 0.5 collective-permute-start.9
  67.1 0.2 collective-permute-start.10
  67.3 0.0 collective-permute-done.1.back
  67.3 0.8 copy-done.5
  68.1 9.6 %shard_map.102 = (f32[4,384,512]{2,1,0:T(8,128)}, bf16[2048,256]{1,0:T(8,128)(2,1)}) custom-call(bf16[4,384,512]{2,1,0:T(8,128)(2,1)} %bitcast.41, bf16[4,384,512]{2,1,0:T(8,128)(2,1)} %bitcast.43, bf16[4,384,256]{2,1,0:T(8,128)(2,1)} %get-tuple-element.17.att, bf16[4,384,256]{2,1,0:T(8,128)(2,1)} %get-tuple-element.18.dq, ...), custom_call_target="tpu_custom_call" | custom-call | flops 5000000000 | bytes 8388608 | tf_op jit(solution)/shard_map/pallas_call | solution.py:350
  77.7 44.4 %shard_map.105 = bf16[2,2048,256]{2,1,0:T(8,128)(2,1)} custom-call(bf16[2048,256]{1,0:T(8,128)(2,1)} %get-tuple-element.27.wt, bf16[2048,256]{1,0:T(8,128)(2,1)} %get-tuple-element.28.ws), custom_call_target="tpu_custom_call" | custom-call | flops 1000000000 | bytes 8388608 | tf_op jit(solution)/shard_map/pallas_call | solution.py:350
  122.2 2.0 %convert_multiply_fusion = f32[2,2048,256]{2,1,0:T(8,128)S(1)} fusion(bf16[2,2048,256]{2,1,0:T(8,128)(2,1)} %shard_map.105), kind=kLoop, calls=%fused_computation | loop fusion | flops 2097152 | bytes 6291456 | tf_op jit(solution)/shard_map/mul | solution.py:454
  124.1 0.4 slice_bitcast_fusion.1
  124.5 1.6 %pad_maximum_fusion = (f32[512,512]{1,0:T(8,128)}, f32[512,512]{1,0:T(8,128)}) fusion(f32[512,256]{1,0:T(8,128)S(1)} %get-tuple-element.37, f32[512,256]{1,0:T(8,128)S(1)} %get-tuple-element.38, f32[512,256]{1,0:T(8,128)S(1)} %get-tuple-element.35, f32[512,256]{1,0:T(8,128)S(1)} %get-tuple-element.36), kind=kLoop, calls=%fused_computation.1 | loop fusion | flops 524288 | bytes 4194304 | tf_op jit(solution)/shard_map/concatenate | solution.py:457
  126.2 0.1 slice_bitcast_fusion.9
  126.3 1.6 %pad_maximum_fusion.2 = (f32[512,512]{1,0:T(8,128)}, f32[512,512]{1,0:T(8,128)}) fusion(f32[512,256]{1,0:T(8,128)S(1)} %get-tuple-element.34, f32[512,256]{1,0:T(8,128)S(1)} %get-tuple-element.33, f32[256,256]{1,0:T(8,128)S(1)} %get-tuple-element.30, f32[256,256]{1,0:T(8,128)S(1)} %get-tuple-element.31, f32[256,256]{1,0:T(8,128)S(1)} %get-tuple-element.32, ...), kind=kLoop, calls=%fused_computation.3 | loop fusion | flops 1048576 | bytes 4194304 | tf_op jit(solution)/shard_map/concatenate | solution.py:457
  127.9 0.0 collective-permute-done.8.p1
  127.9 0.0 collective-permute-done.9.p2
  127.9 0.0 collective-permute-done.10.p3
  127.9 0.0 copy-start.3
  127.9 0.7 copy-done.1
  128.6 0.1 copy-done.2
  128.8 0.1 copy-done.3
  128.9 3.7 %shard_map.104 = bf16[4,384,512]{2,1,0:T(8,128)(2,1)} custom-call(f32[4,384,512]{2,1,0:T(8,128)} %get-tuple-element.22.dx, bf16[4,96,512]{2,1,0:T(8,128)(2,1)} %get-tuple-element.23.p0, bf16[4,96,512]{2,1,0:T(8,128)(2,1)} %copy-done.1, bf16[4,96,512]{2,1,0:T(8,128)(2,1)} %copy-done.2, bf16[4,96,512]{2,1,0:T(8,128)(2,1)} %copy-done.3), custom_call_target="tpu_custom_call" | custom-call | flops 10000000 | bytes 8388608 | tf_op jit(solution)/shard_map/pallas_call | solution.py:350
  (11 shorter events, 0.0 us)
Async XLA Ops:
  0.6 15.1 %copy-start = (bf16[1,4,384,512]{3,2,1,0:T(8,128)(2,1)S(1)}, bf16[1,4,384,512]{3,2,1,0:T(8,128)(2,1)}, u32[]{:S(2)}) copy-start(bf16[1,4,384,512]{3,2,1,0:T(8,128)(2,1)} %param.7) | copy-start | bytes 4718596
  1.8 22.1 %collective-permute-start = (bf16[4,128,512]{2,1,0:T(8,128)(2,1)S(1)}, bf16[4,128,512]{2,1,0:T(8,128)(2,1)S(1)}, u32[]{:S(2)}, u32[]{:S(2)}) collective-permute-start(bf16[4,128,512]{2,1,0:T(8,128)(2,1)S(1)} %slice.96), channel_id=1, source_target_pairs={{0,4},{4,8},{8,12},{12,16},{16,20},{20,24},{24,28},{28,32},{32,36}... | collective-permute-start | bytes 1572872 | tf_op jit(solution)/shard_map/ppermute | solution.py:376
  10.2 12.5 %collective-permute-start.2 = (bf16[4,96,512]{2,1,0:T(8,128)(2,1)S(1)}, bf16[4,96,512]{2,1,0:T(8,128)(2,1)S(1)}, u32[]{:S(2)}, u32[]{:S(2)}) collective-permute-start(bf16[4,96,512]{2,1,0:T(8,128)(2,1)S(1)} %get-tuple-element.44), channel_id=1, source_target_pairs={{0,2},{1,3},{2,0},{3,1},{4,6},{5,7},{6,4},{7,5},{8,10},{9,11},{10,... | collective-permute-start | bytes 1179656 | tf_op jit(solution)/shard_map/ppermute | solution.py:371
  13.1 27.5 %collective-permute-start.3 = (bf16[4,96,512]{2,1,0:T(8,128)(2,1)S(1)}, bf16[4,96,512]{2,1,0:T(8,128)(2,1)S(1)}, u32[]{:S(2)}, u32[]{:S(2)}) collective-permute-start(bf16[4,96,512]{2,1,0:T(8,128)(2,1)S(1)} %get-tuple-element.46), channel_id=1, source_target_pairs={{0,1},{1,2},{2,3},{3,0},{4,5},{5,6},{6,7},{7,4},{8,9},{9,10},{10,1... | collective-permute-start | bytes 1179656 | tf_op jit(solution)/shard_map/ppermute | solution.py:371
  13.5 29.0 %collective-permute-start.4 = (bf16[4,96,512]{2,1,0:T(8,128)(2,1)S(1)}, bf16[4,96,512]{2,1,0:T(8,128)(2,1)S(1)}, u32[]{:S(2)}, u32[]{:S(2)}) collective-permute-start(bf16[4,96,512]{2,1,0:T(8,128)(2,1)S(1)} %get-tuple-element.43), channel_id=1, source_target_pairs={{0,3},{1,0},{2,1},{3,2},{4,7},{5,4},{6,5},{7,6},{8,11},{9,8},{10,9... | collective-permute-start | bytes 1179656 | tf_op jit(solution)/shard_map/ppermute | solution.py:371
  16.7 25.8 %collective-permute-start.5 = (bf16[4,96,512]{2,1,0:T(8,128)(2,1)S(1)}, bf16[4,96,512]{2,1,0:T(8,128)(2,1)S(1)}, u32[]{:S(2)}, u32[]{:S(2)}) collective-permute-start(bf16[4,96,512]{2,1,0:T(8,128)(2,1)S(1)} %get-tuple-element.40), channel_id=1, source_target_pairs={{0,2},{1,3},{2,0},{3,1},{4,6},{5,7},{6,4},{7,5},{8,10},{9,11},{10,... | collective-permute-start | bytes 1179656 | tf_op jit(solution)/shard_map/ppermute | solution.py:371
  22.6 17.9 %copy-start.6 = (bf16[4,96,512]{2,1,0:T(8,128)(2,1)}, bf16[4,96,512]{2,1,0:T(8,128)(2,1)S(1)}, u32[]{:S(2)}) copy-start(bf16[4,96,512]{2,1,0:T(8,128)(2,1)S(1)} %collective-permute-done.2.refs_1_) | copy-start | bytes 1179652
  22.6 22.7 %collective-permute-start.6 = (bf16[4,96,512]{2,1,0:T(8,128)(2,1)S(1)}, bf16[4,96,512]{2,1,0:T(8,128)(2,1)S(1)}, u32[]{:S(2)}, u32[]{:S(2)}) collective-permute-start(bf16[4,96,512]{2,1,0:T(8,128)(2,1)S(1)} %get-tuple-element.42), channel_id=1, source_target_pairs={{0,1},{1,2},{2,3},{3,0},{4,5},{5,6},{6,7},{7,4},{8,9},{9,10},{10,1... | collective-permute-start | bytes 1179656 | tf_op jit(solution)/shard_map/ppermute | solution.py:371
  23.9 1.5 %copy-start.4 = (bf16[4,128,512]{2,1,0:T(8,128)(2,1)}, bf16[4,128,512]{2,1,0:T(8,128)(2,1)S(1)}, u32[]{:S(2)}) copy-start(bf16[4,128,512]{2,1,0:T(8,128)(2,1)S(1)} %collective-permute-done.halo) | copy-start | bytes 1572868
  23.9 22.0 %collective-permute-start.7 = (bf16[4,96,512]{2,1,0:T(8,128)(2,1)S(1)}, bf16[4,96,512]{2,1,0:T(8,128)(2,1)S(1)}, u32[]{:S(2)}, u32[]{:S(2)}) collective-permute-start(bf16[4,96,512]{2,1,0:T(8,128)(2,1)S(1)} %get-tuple-element.39), channel_id=1, source_target_pairs={{0,3},{1,0},{2,1},{3,2},{4,7},{5,4},{6,5},{7,6},{8,11},{9,8},{10,9... | collective-permute-start | bytes 1179656 | tf_op jit(solution)/shard_map/ppermute | solution.py:371
  40.6 5.4 %copy-start.7 = (bf16[4,96,512]{2,1,0:T(8,128)(2,1)}, bf16[4,96,512]{2,1,0:T(8,128)(2,1)S(1)}, u32[]{:S(2)}) copy-start(bf16[4,96,512]{2,1,0:T(8,128)(2,1)S(1)} %collective-permute-done.3.refs_2_) | copy-start | bytes 1179652
  40.6 26.7 %collective-permute-start.1 = (bf16[2,4,128,256]{3,2,1,0:T(8,128)(2,1)}, bf16[2,4,128,256]{3,2,1,0:T(8,128)(2,1)S(1)}, u32[]{:S(2)}, u32[]{:S(2)}) collective-permute-start(bf16[2,4,128,256]{3,2,1,0:T(8,128)(2,1)} %get-tuple-element.21), channel_id=1, source_target_pairs={{4,0},{8,4},{12,8},{16,12},{20,16},{24,20},{28,24},{32,28},{36,32}... | collective-permute-start | bytes 1572872 | tf_op jit(solution)/shard_map/ppermute | solution.py:376
  42.5 3.4 %copy-start.8 = (bf16[4,96,512]{2,1,0:T(8,128)(2,1)}, bf16[4,96,512]{2,1,0:T(8,128)(2,1)S(1)}, u32[]{:S(2)}) copy-start(bf16[4,96,512]{2,1,0:T(8,128)(2,1)S(1)} %collective-permute-done.4.refs_3_) | copy-start | bytes 1179652
  42.5 3.4 %copy-start.9 = (bf16[4,96,512]{2,1,0:T(8,128)(2,1)}, bf16[4,96,512]{2,1,0:T(8,128)(2,1)S(1)}, u32[]{:S(2)}) copy-start(bf16[4,96,512]{2,1,0:T(8,128)(2,1)S(1)} %collective-permute-done.5.refs_5_) | copy-start | bytes 1179652
  45.4 0.7 copy-start.10
  45.9 0.8 copy-start.11
  64.1 63.8 %collective-permute-start.8 = (bf16[4,96,512]{2,1,0:T(8,128)(2,1)}, bf16[4,96,512]{2,1,0:T(8,128)(2,1)S(1)}, u32[]{:S(2)}, u32[]{:S(2)}) collective-permute-start(bf16[4,96,512]{2,1,0:T(8,128)(2,1)} %get-tuple-element.24), channel_id=1, source_target_pairs={{0,3},{1,0},{2,1},{3,2},{4,7},{5,4},{6,5},{7,6},{8,11},{9,8},{10,9... | collective-permute-start | bytes 1179656 | tf_op jit(solution)/shard_map/ppermute | solution.py:371
  66.6 61.3 %collective-permute-start.9 = (bf16[4,96,512]{2,1,0:T(8,128)(2,1)}, bf16[4,96,512]{2,1,0:T(8,128)(2,1)S(1)}, u32[]{:S(2)}, u32[]{:S(2)}) collective-permute-start(bf16[4,96,512]{2,1,0:T(8,128)(2,1)} %get-tuple-element.25), channel_id=1, source_target_pairs={{0,2},{1,3},{2,0},{3,1},{4,6},{5,7},{6,4},{7,5},{8,10},{9,11},{10,... | collective-permute-start | bytes 1179656 | tf_op jit(solution)/shard_map/ppermute | solution.py:371
  67.1 60.9 %collective-permute-start.10 = (bf16[4,96,512]{2,1,0:T(8,128)(2,1)}, bf16[4,96,512]{2,1,0:T(8,128)(2,1)S(1)}, u32[]{:S(2)}, u32[]{:S(2)}) collective-permute-start(bf16[4,96,512]{2,1,0:T(8,128)(2,1)} %get-tuple-element.26), channel_id=1, source_target_pairs={{0,1},{1,2},{2,3},{3,0},{4,5},{5,6},{6,7},{7,4},{8,9},{9,10},{10,1... | collective-permute-start | bytes 1179656 | tf_op jit(solution)/shard_map/ppermute | solution.py:371
  67.3 0.8 copy-start.5
  127.9 0.7 copy-start.1
  127.9 0.9 copy-start.2
  127.9 1.0 copy-start.3
where the time goes:
time: 133 us
  Pallas kernels  90.3 us (68%)
  starting transfers between devices  19.5 us (15%)
  waiting for transfers between devices  9.33 us (7%)
  local copies, waits for them, and re-layouts  7.43 us (6%)
  other arithmetic  5.25 us (4%)
    pallas_call x5, Pallas kernels, run(): pl.pallas_call(kernel, out_shape=outs, in_specs=[pl.BlockSpec(memory_spac...  90.3 us
    ppermute x9, starting transfers between devices, rotate(): lax.ppermute(block, axis, [(i, (i + distance) % count) for i in range(cou...  11.6 us
    ppermute x9, waiting for transfers between devices, rotate(): lax.ppermute(block, axis, [(i, (i + distance) % count) for i in range(cou...  9.32 us
    ppermute x2, starting transfers between devices, shifted(): lax.ppermute(block, axis, [(i - distance, i) for i in devices if i - dist...  7.96 us
    concatenate x2, other arithmetic, shards(): jnp.concatenate([space[i:i + 512], time[i:i + 512]], axis=1)  3.28 us
    dynamic_slice x2, local copies, waits for them, and re-layouts, piece(): return lax.dynamic_slice_in_dim(t, lax.rem(me + d, 4) * quarter, quarter, 1)  3.17 us
  transfers between devices with their start and end apart: 11, of which 3 were waited for; matrix products, arithmetic and copies ran while one was open for 7% of the time, Pallas kernels for 65%

commit v1 on v0

v1 whole, which is shorter than its diff:
```python
import math

import jax
import jax.numpy as jnp
from jax import lax
from jax.experimental import pallas as pl
from jax.experimental.pallas import tpu as pltpu
from jax.sharding import PartitionSpec as P

BF16 = jnp.bfloat16
F32 = jnp.float32
WIN = 128
HALF = 256
HEAD = 64
HEADS = 4
NEG = -1e30
SCALE = 0.125
VMEM_LIMIT = 56 * 1024 * 1024
MESH = pl.DeviceIdType.MESH

NN = (((1,), (0,)), ((), ()))
NT = (((1,), (1,)), ((), ()))
TN = (((0,), (0,)), ((), ()))


def mm(left, right, dims):
    return lax.dot_general(left, right, dims, preferred_element_type=F32)


def stack_heads(rows):
    head = lax.broadcasted_iota(jnp.int32, (1, HALF), 1) // HEAD
    return jnp.concatenate(
        [rows * (head == h).astype(F32).astype(BF16) for h in range(HEADS)], axis=0
    )


def pick_heads(rows):
    count = rows.shape[0] // HEADS
    head = lax.broadcasted_iota(jnp.int32, (count, HALF), 1) // HEAD
    out = rows[:count]
    for h in range(1, HEADS):
        out = jnp.where(head == h, rows[h * count : (h + 1) * count], out)
    return out


def soft(scores, grad_probs):
    peak = jnp.max(scores, axis=0, keepdims=True)
    ex = jnp.exp(scores - peak)
    probs = ex / jnp.sum(ex, axis=0, keepdims=True)
    delta = jnp.sum(probs * grad_probs, axis=0, keepdims=True)
    return probs, probs * (grad_probs - delta)


def temporal_block(q, ga, k, v, bias):
    qs, gs = stack_heads(q), stack_heads(ga)
    st = mm(k, qs, NT)
    gt = mm(v, gs, NT)
    shape = (WIN, HEADS * WIN)
    older = lax.broadcasted_iota(jnp.int32, shape, 0) > lax.rem(
        lax.broadcasted_iota(jnp.int32, shape, 1), WIN
    )
    probs, grad = soft(
        jnp.where(older, st[:WIN] + bias, st[WIN:]), jnp.where(older, gt[:WIN], gt[WIN:])
    )

    def spread(t):
        return jnp.concatenate(
            [jnp.where(older, t, 0.0).astype(BF16), jnp.where(older, 0.0, t).astype(BF16)], axis=0
        )

    pt, dt = spread(probs), spread(grad)
    att = pick_heads(mm(pt, v, TN))
    dq = pick_heads(mm(dt, k, TN)) * SCALE
    return att, dq, mm(dt, qs, NN), mm(pt, gs, NN)


def spatial_block(q, ga, k, v):
    qs, gs = stack_heads(q), stack_heads(ga)
    shape = (WIN, HEADS * WIN)
    same = lax.rem(lax.broadcasted_iota(jnp.int32, shape, 0), 8) == lax.rem(
        lax.broadcasted_iota(jnp.int32, shape, 1), 8
    )
    probs, grad = soft(jnp.where(same, mm(k, qs, NT), NEG), mm(v, gs, NT))
    pt, dt = probs.astype(BF16), grad.astype(BF16)
    att = pick_heads(mm(pt, v, TN))
    dq = pick_heads(mm(dt, k, TN)) * SCALE
    return att, dq, mm(dt, qs, NN), mm(pt, gs, NN)


def coordinates():
    dp, tm, y = lax.axis_index("dp"), lax.axis_index("tm"), lax.axis_index("elec")
    z, rest = lax.div(tm, 4), lax.rem(tm, 4)
    x = lax.div(rest, 2) * 2 + dp
    return x, y, z, lax.rem(rest, 2)


def device_at(x, y, z, core):
    return {"dp": lax.rem(x, 2), "tm": z * 4 + lax.div(x, 2) * 2 + core, "elec": y}


CHUNKS = 3
STEPS = 20


def weight_rows(acc_in, acc_out, dst):
    for j in range(2):
        for i in range(3):
            first = i * HALF + j * 128
            dst[j, i * 512 : (i + 1) * 512] = acc_in[:, first : first + 128].astype(BF16)
        for i in range(2):
            first = i * HALF + j * 128
            dst[j, 1536 + i * HALF : 1536 + (i + 1) * HALF] = acc_out[:, first : first + 128].astype(BF16)


def layer_kernel(x_h, cot_h, wq_h, wk_h, wv_h, wo_h, out, *rest):
    w_outs = rest[:4]
    (
        xv, cv, halo, w_t, w_s, wo, q_t, k_t, v_t, g_t, dk_t, dv_t, att_t, dq_t, back_out, back_in, dx_t,
        xr, cr, q_s, k_s, v_s, g_s, dxs, dxr, acc_in_t, acc_out_t, acc_in_s, acc_out_s,
        ar_src, recv_c, part_c, recv_a, part_a, recv_b, part_b, recv_e, ar_out,
        load_sem, halo_send, halo_recv, go_send, go_recv, ret_send, ret_recv, ar_send, ar_recv,
    ) = rest[4:]
    elecs, patches, width = xv.shape
    quarter = patches // 4
    chunk = quarter // CHUNKS
    x, y, z, core = coordinates()
    tm = lax.axis_index("tm")
    right = {"tm": lax.rem(tm + 1, 16)}
    left = {"tm": lax.rem(tm + 15, 16)}
    other_core = device_at(x, y, z, 1 - core)
    where = {"x": x, "y": y, "z": z}

    def peer(axis, d):
        if axis == "x":
            return device_at(lax.rem(x + d, 4), y, z, core)
        if axis == "y":
            return {"elec": lax.rem(y + d, 4)}
        return device_at(x, y, lax.rem(z + d, 4), core)

    barrier = pltpu.get_barrier_semaphore()
    for device in [right, left, other_core] + [peer(axis, d) for axis in "xyz" for d in range(1, 4)]:
        pl.semaphore_signal(barrier, inc=1, device_id=device, device_id_type=MESH)
    pl.semaphore_wait(barrier, 12)

    sent = []

    def send(src, dst, send_sem, recv_sem, device):
        copy = pltpu.make_async_remote_copy(
            src_ref=src, dst_ref=dst, send_sem=send_sem, recv_sem=recv_sem, device_id=device, device_id_type=MESH
        )
        copy.start()
        sent.append(copy)
        return copy

    def rows_at(first, size):
        return pl.ds(pl.multiple_of(first, 16), size)

    halo_copy = send(x_h.at[:, patches - WIN :], halo, halo_send.at[0], halo_recv.at[0], right)
    loads = []

    def load(src, dst):
        copy = pltpu.make_async_copy(src, dst, load_sem.at[len(loads)])
        copy.start()
        loads.append(copy)

    load(x_h, xv)
    load(cot_h, cv)
    load(wo_h, wo)
    for i, w in enumerate((wq_h, wk_h, wv_h)):
        load(w.at[:, HALF:], w_t.at[:, i * HALF : (i + 1) * HALF])
    go = {}
    for c in range(CHUNKS):
        for d in (2, 1, 3):
            at = rows_at(lax.rem(y + d, 4) * quarter + c * chunk, chunk)
            slot = slice(d * elecs, (d + 1) * elecs)
            go[c, d] = [
                send(src.at[:, at], dst.at[c, slot], go_send.at[c, d - 1, k], go_recv.at[c, d - 1, k], peer("y", d))
                for k, (src, dst) in enumerate(((x_h, xr), (cot_h, cr)))
            ]
    for i, w in enumerate((wq_h, wk_h, wv_h)):
        load(w.at[:, :HALF], w_s.at[:, i * HALF : (i + 1) * HALF])
    for c in range(CHUNKS):
        at = rows_at(y * quarter + c * chunk, chunk)
        load(x_h.at[:, at], xr.at[c, :elecs])
        load(cot_h.at[:, at], cr.at[c, :elecs])
    for copy in loads:
        copy.wait()

    bias0 = jnp.where(tm == 0, NEG, 0.0).astype(F32)

    def project_time(e, carry):
        q_t[e] = (mm(xv[e], w_t[:, :HALF], NN) * SCALE).astype(BF16)
        k_t[e, WIN:] = mm(xv[e], w_t[:, HALF : 2 * HALF], NN).astype(BF16)
        v_t[e, WIN:] = mm(xv[e], w_t[:, 2 * HALF :], NN).astype(BF16)
        g_t[e] = mm(cv[e], wo[HALF:, :], NT).astype(BF16)
        return carry

    lax.fori_loop(0, elecs, project_time, 0)

    def time_block(e, c, bias):
        rows, keys = slice(c * WIN, (c + 1) * WIN), slice(c * WIN, (c + 2) * WIN)
        att, dq, dk, dv = temporal_block(q_t[e, rows], g_t[e, rows], k_t[e, keys], v_t[e, keys], bias)
        att_t[e, rows] = att.astype(BF16)
        dq_t[e, rows] = dq.astype(BF16)
        return dk, dv

    def later_blocks(e, carry):
        ones = time_block(e, 1, 0.0)
        twos = time_block(e, 2, 0.0)
        for ref, one, two in zip((dk_t, dv_t), ones, twos):
            ref[e, :WIN] = one[:WIN]
            ref[e, WIN : 2 * WIN] = one[WIN:] + two[:WIN]
            ref[e, 2 * WIN :] = two[WIN:]
        return carry

    lax.fori_loop(0, elecs, later_blocks, 0)
    halo_copy.wait_recv()

    def first_blocks(i, carry):
        for e in (2 * i, 2 * i + 1):
            k_t[e, :WIN] = mm(halo[e], w_t[:, HALF : 2 * HALF], NN).astype(BF16)
            v_t[e, :WIN] = mm(halo[e], w_t[:, 2 * HALF :], NN).astype(BF16)
            for side, (ref, grad) in enumerate(zip((dk_t, dv_t), time_block(e, 0, bias0))):
                back_out[side, e] = grad[:WIN].astype(BF16)
                ref[e, :WIN] += grad[WIN:]
        return carry

    lax.fori_loop(0, elecs // 2, first_blocks, 0)
    back_copy = send(back_out, back_in, halo_send.at[1], halo_recv.at[1], left)

    rows = 4 * elecs * chunk

    def spatial_project(c):
        for d in range(1, 4):
            for copy in go[c, d]:
                copy.wait_recv()
        xi = xr[c].reshape(rows, width)
        shape = (4 * elecs, chunk, HALF)
        q_s[...] = (mm(xi, w_s[:, :HALF], NN) * SCALE).reshape(shape)
        k_s[...] = mm(xi, w_s[:, HALF : 2 * HALF], NN).reshape(shape)
        v_s[...] = mm(xi, w_s[:, 2 * HALF :], NN).reshape(shape)
        g_s[...] = mm(cr[c].reshape(rows, width), wo[:HALF, :], NT).reshape(shape)

    def spatial_attend():
        def block(i, carry):
            for j in range(2):
                at = pl.ds(pl.multiple_of(i * 16 + j * 8, 8), 8)
                q, g, k, v = [ref[:, at, :].reshape(WIN, HALF).astype(BF16) for ref in (q_s, g_s, k_s, v_s)]
                for ref, value in zip((g_s, q_s, k_s, v_s), spatial_block(q, g, k, v)):
                    ref[:, at, :] = value.reshape(4 * elecs, 8, HALF)
            return carry

        lax.fori_loop(0, chunk // 16, block, 0)

    def spatial_end(c):
        xi = xr[c].reshape(rows, width)
        grads = jnp.concatenate([ref[...].astype(BF16).reshape(rows, HALF) for ref in (q_s, k_s, v_s)], axis=1)
        dxs[c] = mm(grads, w_s[...], NT).astype(BF16).reshape(4 * elecs, chunk, width)
        add_in = mm(xi, grads, TN)
        add_out = mm(g_s[...].astype(BF16).reshape(rows, HALF), cr[c].reshape(rows, width), TN)
        if c == 0:
            acc_in_s[...] = add_in
            acc_out_s[...] = add_out
        else:
            acc_in_s[...] += add_in
            acc_out_s[...] += add_out

    returned = {}

    def send_back(c):
        for d in (2, 1, 3):
            slot = slice(d * elecs, (d + 1) * elecs)
            returned[c, d] = send(
                dxs.at[c, slot], dxr.at[c, d - 1], ret_send.at[c, d - 1], ret_recv.at[c, d - 1], peer("y", 4 - d)
            )

    def place(c):
        for d in range(4):
            at = rows_at(lax.rem(y + d, 4) * quarter + c * chunk, chunk)
            if d == 0:
                piece = dxs[c, :elecs]
            else:
                returned[c, d].wait_recv()
                piece = dxr[c, d - 1]
            out[:, at, :] = (dx_t[:, at, :] + piece.astype(F32)).astype(BF16)

    def summing(n):
        orders = ("xzy", "zxy")

        def start(p, step, src, dst, device):
            return send(src, dst, ar_send.at[n, p, step], ar_recv.at[n, p, step], device)

        src = ar_src.at[n]
        waiting = [
            [start(p, 0, src.at[p, rows_at((1 - core) * 1024, 1024)], recv_c.at[n, p], other_core)] for p in range(2)
        ]
        yield
        base = [core * 1024, core * 1024]
        size = 1024
        stages = ((recv_a, part_c), (recv_b, part_a), (recv_e, part_b))
        for stage in range(3):
            size = size // 4
            landing, held = stages[stage]
            for p in range(2):
                for copy in waiting[p]:
                    copy.wait_recv()
                if stage == 0:
                    total = src[p, rows_at(core * 1024, 1024)].astype(F32) + recv_c[n, p].astype(F32)
                else:
                    arrived, before = stages[stage - 1]
                    spot = where[orders[p][stage - 1]]
                    total = before[n, p, rows_at(spot * size * 4, size * 4)].astype(F32)
                    for d in range(3):
                        total = total + arrived[n, p, d].astype(F32)
                held[n, p] = total.astype(BF16)
                axis = orders[p][stage]
                waiting[p] = [
                    start(
                        p,
                        stage * 3 + d,
                        held.at[n, p, rows_at(lax.rem(where[axis] + d, 4) * size, size)],
                        landing.at[n, p, d - 1],
                        peer(axis, d),
                    )
                    for d in range(1, 4)
                ]
                base[p] = base[p] + where[axis] * size
            yield
        for stage in (2, 1, 0):
            for p in range(2):
                for copy in waiting[p]:
                    copy.wait_recv()
                if stage == 2:
                    total = part_b[n, p, rows_at(where["y"] * 16, 16)].astype(F32)
                    for d in range(3):
                        total = total + recv_e[n, p, d].astype(F32)
                    ar_out[n, p, rows_at(base[p], 16)] = total.astype(BF16)
                axis = orders[p][stage]
                spot = ar_out.at[n, p, rows_at(base[p], size)]
                waiting[p] = [start(p, 9 + stage * 3 + d, spot, spot, peer(axis, d)) for d in range(1, 4)]
                base[p] = base[p] - where[axis] * size
            size = size * 4
            yield
        for p in range(2):
            for copy in waiting[p]:
                copy.wait_recv()
            spot = ar_out.at[n, p, rows_at(core * 1024, 1024)]
            waiting[p] = [start(p, 19, spot, spot, other_core)]
        yield
        for p in range(2):
            for copy in waiting[p]:
                copy.wait_recv()
            first = (1 - n) * HALF + p * 128
            for i in range(3):
                w_outs[i][:, first : first + 128] = ar_out[n, p, i * 512 : (i + 1) * 512]
            for i in range(2):
                low, left_col = (1 - n) * HALF, i * HALF + p * 128
                w_outs[3][low : low + HALF, left_col : left_col + 128] = ar_out[
                    n, p, 1536 + i * HALF : 1536 + (i + 1) * HALF
                ]
        yield

    spatial_project(0)
    spatial_attend()
    spatial_end(0)

    back_copy.wait_recv()
    acc_in_t[...] = jnp.zeros_like(acc_in_t)
    acc_out_t[...] = jnp.zeros_like(acc_out_t)

    def end_time(e, carry):
        def full(own, side):
            tail = own[e, patches - WIN :] + back_in[side, e].astype(F32)
            return jnp.concatenate([own[e, : patches - WIN].astype(BF16), tail.astype(BF16)], axis=0)

        grads = jnp.concatenate([dq_t[e], full(dk_t, 0), full(dv_t, 1)], axis=1)
        dx_t[e] = mm(grads, w_t[...], NT)
        acc_in_t[...] += mm(xv[e], grads, TN)
        acc_out_t[...] += mm(att_t[e], cv[e], TN)
        return carry

    lax.fori_loop(0, elecs, end_time, 0)
    weight_rows(acc_in_t, acc_out_t, ar_src.at[0])
    time_sum, space_sum = summing(0), summing(1)
    next(time_sum)
    spatial_project(1)
    next(time_sum)
    spatial_attend()
    next(time_sum)
    spatial_end(1)
    next(time_sum)
    spatial_project(2)
    send_back(0)
    send_back(1)
    next(time_sum)
    spatial_attend()
    next(time_sum)
    spatial_end(2)
    weight_rows(acc_in_s, acc_out_s, ar_src.at[1])
    next(space_sum)
    send_back(2)
    next(time_sum)
    next(space_sum)
    next(time_sum)
    next(space_sum)
    place(0)
    next(time_sum)
    next(space_sum)
    place(1)
    next(space_sum)
    place(2)
    for _ in space_sum:
        pass
    for copy in sent:
        copy.wait_send()


def sds(shape, dtype):
    return jax.ShapeDtypeStruct(shape, dtype)


def shards(inputs, cotangent, w_query, w_key, w_value, w_out):
    _, elecs, patches, width = inputs.shape
    chunk = patches // 4 // CHUNKS
    vm, dma = pltpu.VMEM, pltpu.SemaphoreType.DMA
    tokens = (elecs, patches)
    ext = (elecs, patches + WIN)
    everyone = (4 * elecs, chunk)
    scratch = (
        [vm(tokens + (width,), BF16)] * 2
        + [vm((elecs, WIN, width), BF16)]
        + [vm((width, 3 * HALF), BF16)] * 2
        + [vm((width, width), BF16)]
        + [vm(tokens + (HALF,), BF16), vm(ext + (HALF,), BF16), vm(ext + (HALF,), BF16), vm(tokens + (HALF,), BF16)]
        + [vm(tokens + (HALF,), F32)] * 2
        + [vm(tokens + (HALF,), BF16)] * 2
        + [vm((2, elecs, WIN, HALF), BF16)] * 2
        + [vm(tokens + (width,), F32)]
        + [vm((CHUNKS,) + everyone + (width,), BF16)] * 2
        + [vm(everyone + (HALF,), F32)] * 4
        + [vm((CHUNKS,) + everyone + (width,), BF16), vm((CHUNKS, 3, elecs, chunk, width), BF16)]
        + [vm((width, 3 * HALF), F32), vm((HALF, width), F32)] * 2
        + [vm((2, 2, 2048, 128), BF16)]
        + [vm((2, 2, 1024, 128), BF16)] * 2
        + [vm((2, 2, 3, 256, 128), BF16), vm((2, 2, 256, 128), BF16)]
        + [vm((2, 2, 3, 64, 128), BF16), vm((2, 2, 64, 128), BF16)]
        + [vm((2, 2, 3, 16, 128), BF16)]
        + [vm((2, 2, 2048, 128), BF16)]
        + [dma((6 + 3 + 2 * CHUNKS,)), dma((2,)), dma((2,))]
        + [dma((CHUNKS, 3, 2))] * 2
        + [dma((CHUNKS, 3))] * 2
        + [dma((2, 2, STEPS))] * 2
    )
    grad_inputs, *grads = pl.pallas_call(
        layer_kernel,
        out_shape=(sds(tokens + (width,), BF16),) + (sds((width, width), BF16),) * 4,
        in_specs=[pl.BlockSpec(memory_space=pl.ANY)] * 6,
        out_specs=(pl.BlockSpec(memory_space=pltpu.VMEM),) * 5,
        scratch_shapes=scratch,
        compiler_params=pltpu.CompilerParams(
            collective_id=0, has_side_effects=True, vmem_limit_bytes=VMEM_LIMIT
        ),
        cost_estimate=pl.CostEstimate(flops=2 * 10**10, bytes_accessed=10**7, transcendentals=2 * 10**6),
    )(inputs[0], cotangent[0], w_query, w_key, w_value, w_out)
    norm = 1.0 / math.sqrt(196608)
    return (grad_inputs[None],) + tuple(grad.astype(F32) * norm for grad in grads)


def solution(mesh):
    return jax.shard_map(
        shards,
        mesh=mesh,
        in_specs=(P("dp", "elec", "tm", None), P("dp", "elec", "tm", None), P(), P(), P(), P()),
        out_specs=(P("dp", "elec", "tm", None), P(), P(), P(), P()),
        check_vma=False,
    )
```

time: 133 us -> 102 us (0.77)
  starting transfers between devices: 19.5 us -> 0 us
  waiting for transfers between devices: 9.33 us -> 0 us
  local copies, waits for them, and re-layouts: 7.43 us -> 1.29 us
  Pallas kernels: 90.3 us -> 95.2 us
    ppermute x11 -> x0, starting transfers between devices: 19.5 us -> none  [the longest x9 11.6 us: rotate(): lax.ppermute(block, axis, [(i, (i + distance) % count) for i in range(cou...]
    ppermute x11 -> x0, waiting for transfers between devices: 9.33 us -> none  [the longest x9 9.32 us: rotate(): lax.ppermute(block, axis, [(i, (i + distance) % count) for i in range(cou...]
    pallas_call x5 -> x1, Pallas kernels: 90.3 us -> 95.2 us  [shards(): pl.pallas_call(layer_kernel, out_shape=(sds(tokens + (width,), BF16),) +...]
    concatenate x2 -> x0, other arithmetic: 3.28 us -> none  [shards(): jnp.concatenate([space[i:i + 512], time[i:i + 512]], axis=1)]
    dynamic_slice x2 -> x0, local copies, waits for them, and re-layouts: 3.17 us -> none  [piece(): return lax.dynamic_slice_in_dim(t, lax.rem(me + d, 4) * quarter, quarter, 1)]
    mul x1 -> x2, other arithmetic: 1.96 us -> 4.52 us  [shards(): grad.astype(F32) * norm]
    slice x3 -> x0, local copies, waits for them, and re-layouts: 1.66 us -> none  [the longest x1 1.2 us: shards(): halo = shifted(x[:, patches - WIN:], 'tm', 1)]
  transfers between devices with their start and end apart: 11 -> 0, of which waited for: 3 -> 0; matrix products, arithmetic and copies ran while one was open for 7% -> 0% of each run, Pallas kernels for 65% -> 0%
where the time goes in v1:
time: 102 us
  Pallas kernels  95.2 us (93%)
  other arithmetic  4.52 us (4%)
  local copies, waits for them, and re-layouts  1.29 us (1%)
    pallas_call x1, Pallas kernels, shards(): pl.pallas_call(layer_kernel, out_shape=(sds(tokens + (width,), BF16),) +...  95.2 us
    mul x2, other arithmetic, shards(): grad.astype(F32) * norm  4.52 us

profile of v1, /device:TPU:1, one launch (start us, length us, event | category | flops | bytes accessed | tf_op | source)
XLA Modules:
  0.0 101.7 jit_solution(2738868990108913034)
XLA Ops:
  0.6 95.2 %shard_map.101 = (bf16[4,384,512]{2,1,0:T(8,128)(2,1)}, bf16[512,512]{1,0:T(8,128)(2,1)}, bf16[512,512]{1,0:T(8,128)(2,1)}, bf16[512,512]{1,0:T(8,128)(2,1)}, bf16[512,512]{1,0:T(8,128)(2,1)}) custom-call(bf16[4,384,512]{2,1,0:T(8,128)(2,1)} %bitcast.4, bf16[4,384,512]{2,1,0:T(8,128)(2,1)} %bitcast.5, bf16[512,512]{1,0:T(8,128)(2,1)} %wq_h.1, ...), custom_call_target="tpu_custom_call" | custom-call | flops 20000000000 | bytes 10000000 | tf_op jit(solution)/shard_map/pallas_call | solution.py:454
  95.9 0.0 copy-start.1
  95.9 0.0 copy-start.2
  95.9 2.9 %convert_multiply_fusion.2 = (f32[512,512]{1,0:T(8,128)}, f32[512,512]{1,0:T(8,128)}) fusion(bf16[512,512]{1,0:T(8,128)(2,1)} %get-tuple-element.12, bf16[512,512]{1,0:T(8,128)(2,1)} %get-tuple-element.11), kind=kLoop, calls=%fused_computation.2 | loop fusion | flops 1048576 | bytes 3145728 | tf_op jit(solution)/shard_map/mul | solution.py:466
  98.8 0.0 copy-done.1
  98.8 0.0 copy-done.2
  98.8 0.0 copy-start
  98.8 1.6 %convert_multiply_fusion = (f32[512,512]{1,0:T(8,128)}, f32[512,512]{1,0:T(8,128)}) fusion(bf16[512,512]{1,0:T(8,128)(2,1)S(1)} %copy-done.2, bf16[512,512]{1,0:T(8,128)(2,1)S(1)} %copy-done.1), kind=kLoop, calls=%fused_computation | loop fusion | flops 1048576 | bytes 3145728 | tf_op jit(solution)/shard_map/mul | solution.py:466
  100.4 0.1 copy-done
  100.6 1.1 %copy.12 = bf16[1,4,384,512]{3,2,1,0:T(8,128)(2,1)} copy(bf16[1,4,384,512]{3,2,1,0:T(8,128)(2,1)S(1)} %bitcast.3) | data formatting | bytes 3145728
Async XLA Ops:
  95.9 2.9 %copy-start.1 = (bf16[512,512]{1,0:T(8,128)(2,1)S(1)}, bf16[512,512]{1,0:T(8,128)(2,1)}, u32[]{:S(2)}) copy-start(bf16[512,512]{1,0:T(8,128)(2,1)} %get-tuple-element.13) | copy-start | bytes 1572868
  95.9 2.9 %copy-start.2 = (bf16[512,512]{1,0:T(8,128)(2,1)S(1)}, bf16[512,512]{1,0:T(8,128)(2,1)}, u32[]{:S(2)}) copy-start(bf16[512,512]{1,0:T(8,128)(2,1)} %get-tuple-element.14) | copy-start | bytes 1572868
  98.8 1.8 %copy-start = (bf16[4,384,512]{2,1,0:T(8,128)(2,1)S(1)}, bf16[4,384,512]{2,1,0:T(8,128)(2,1)}, u32[]{:S(2)}) copy-start(bf16[4,384,512]{2,1,0:T(8,128)(2,1)} %get-tuple-element.10) | copy-start | bytes 4718596

commit v2 on v1

v2 whole, which is shorter than its diff:
```python
import math

import jax
import jax.numpy as jnp
from jax import lax
from jax.experimental import pallas as pl
from jax.experimental.pallas import tpu as pltpu
from jax.sharding import PartitionSpec as P

BF16 = jnp.bfloat16
F32 = jnp.float32
WIN = 128
HALF = 256
HEAD = 64
HEADS = 4
NEG = -1e30
SCALE = 0.125
VMEM_LIMIT = 56 * 1024 * 1024
MESH = pl.DeviceIdType.MESH

NN = (((1,), (0,)), ((), ()))
NT = (((1,), (1,)), ((), ()))
TN = (((0,), (0,)), ((), ()))


def mm(left, right, dims):
    return lax.dot_general(left, right, dims, preferred_element_type=F32)


def stack_heads(rows):
    head = lax.broadcasted_iota(jnp.int32, (1, HALF), 1) // HEAD
    return jnp.concatenate(
        [rows * (head == h).astype(F32).astype(BF16) for h in range(HEADS)], axis=0
    )


def pick_heads(rows):
    count = rows.shape[0] // HEADS
    head = lax.broadcasted_iota(jnp.int32, (count, HALF), 1) // HEAD
    out = rows[:count]
    for h in range(1, HEADS):
        out = jnp.where(head == h, rows[h * count : (h + 1) * count], out)
    return out


def soft(scores, grad_probs):
    peak = jnp.max(scores, axis=0, keepdims=True)
    ex = jnp.exp(scores - peak)
    probs = ex / jnp.sum(ex, axis=0, keepdims=True)
    delta = jnp.sum(probs * grad_probs, axis=0, keepdims=True)
    return probs, probs * (grad_probs - delta)


def temporal_block(q, ga, k, v, bias):
    qs, gs = stack_heads(q), stack_heads(ga)
    st = mm(k, qs, NT)
    gt = mm(v, gs, NT)
    shape = (WIN, HEADS * WIN)
    older = lax.broadcasted_iota(jnp.int32, shape, 0) > lax.rem(
        lax.broadcasted_iota(jnp.int32, shape, 1), WIN
    )
    probs, grad = soft(
        jnp.where(older, st[:WIN] + bias, st[WIN:]), jnp.where(older, gt[:WIN], gt[WIN:])
    )

    def spread(t):
        return jnp.concatenate(
            [jnp.where(older, t, 0.0).astype(BF16), jnp.where(older, 0.0, t).astype(BF16)], axis=0
        )

    pt, dt = spread(probs), spread(grad)
    att = pick_heads(mm(pt, v, TN))
    dq = pick_heads(mm(dt, k, TN)) * SCALE
    return att, dq, mm(dt, qs, NN), mm(pt, gs, NN)


def spatial_block(q, ga, k, v):
    qs, gs = stack_heads(q), stack_heads(ga)
    shape = (WIN, HEADS * WIN)
    same = lax.rem(lax.broadcasted_iota(jnp.int32, shape, 0), 8) == lax.rem(
        lax.broadcasted_iota(jnp.int32, shape, 1), 8
    )
    probs, grad = soft(jnp.where(same, mm(k, qs, NT), NEG), mm(v, gs, NT))
    pt, dt = probs.astype(BF16), grad.astype(BF16)
    att = pick_heads(mm(pt, v, TN))
    dq = pick_heads(mm(dt, k, TN)) * SCALE
    return att, dq, mm(dt, qs, NN), mm(pt, gs, NN)


def coordinates():
    dp, tm, y = lax.axis_index("dp"), lax.axis_index("tm"), lax.axis_index("elec")
    z, rest = lax.div(tm, 4), lax.rem(tm, 4)
    x = lax.div(rest, 2) * 2 + dp
    return x, y, z, lax.rem(rest, 2)


def device_at(x, y, z, core):
    return {"dp": lax.rem(x, 2), "tm": z * 4 + lax.div(x, 2) * 2 + core, "elec": y}


CHUNKS = (48, 32, 16)
STARTS = (0, 48, 80)


def weight_rows(acc_in, acc_out, dst):
    for j in range(2):
        for i in range(3):
            first = i * HALF + j * 128
            dst[j, i * 512 : (i + 1) * 512] = acc_in[:, first : first + 128].astype(BF16)
        for i in range(2):
            first = i * HALF + j * 128
            dst[j, 1536 + i * HALF : 1536 + (i + 1) * HALF] = acc_out[:, first : first + 128].astype(BF16)


def layer_kernel(x_h, cot_h, wq_h, wk_h, wv_h, wo_h, out, *rest):
    w_outs = rest[:4]
    (
        xv, cv, halo, w_t, w_s, wo, q_t, k_t, v_t, g_t, dk_t, dv_t, att_t, dq_t, back_out, back_in, dx_t,
        xr, cr, q_s, k_s, v_s, g_s, dxs, dxr, acc_in_t, acc_out_t, acc_in_s, acc_out_s,
        ar_src, recv_a, part, recv_b, ar_out,
        load_sem, halo_send, halo_recv, go_send, go_recv, ret_send, ret_recv, ar_send, ar_recv,
    ) = rest[4:]
    elecs, patches, width = xv.shape
    quarter = patches // 4
    x, y, z, core = coordinates()
    tm = lax.axis_index("tm")
    right = {"tm": lax.rem(tm + 1, 16)}
    left = {"tm": lax.rem(tm + 15, 16)}
    where = {"x": x, "y": y, "z": z, "core": core}

    def peer(**by):
        at = {n: lax.rem(where[n] + by.get(n, 0), 2 if n == "core" else 4) for n in where}
        return device_at(at["x"], at["y"], at["z"], at["core"])

    orders = ((("x", "core"), ("z", "y")), (("z", "core"), ("x", "y")))

    def others(axes):
        low = 2 if axes[1] == "core" else 4
        return [(i, {axes[0]: i // low, axes[1]: i % low}) for i in range(1, 4 * low)]

    near = {tuple(sorted(by.items())) for axes in (orders[0] + orders[1]) for _, by in others(axes)}
    near = sorted({tuple((n, v) for n, v in by if v) for by in near})
    barrier = pltpu.get_barrier_semaphore()
    for device in [right, left] + [peer(**dict(by)) for by in near]:
        pl.semaphore_signal(barrier, inc=1, device_id=device, device_id_type=MESH)
    pl.semaphore_wait(barrier, 2 + len(near))

    pending = []

    def push(src, dst, sems, device):
        pltpu.make_async_remote_copy(
            src_ref=src, dst_ref=dst, send_sem=sems[0], recv_sem=sems[1], device_id=device, device_id_type=MESH
        ).start()

    def group(ref, sems):
        whole = pltpu.make_async_remote_copy(
            src_ref=ref, dst_ref=ref, send_sem=sems[0], recv_sem=sems[1], device_id=right, device_id_type=MESH
        )
        pending.append(whole)
        return whole

    def rows_at(first, size):
        return pl.ds(pl.multiple_of(first, 16), size)

    loads = []

    def load(src, dst):
        copy = pltpu.make_async_copy(src, dst, load_sem.at[len(loads)])
        copy.start()
        loads.append(copy)

    load(x_h, xv)
    load(cot_h, cv)
    load(wo_h, wo)
    for i, w in enumerate((wq_h, wk_h, wv_h)):
        load(w.at[:, HALF:], w_t.at[:, i * HALF : (i + 1) * HALF])
    for i, w in enumerate((wq_h, wk_h, wv_h)):
        load(w.at[:, :HALF], w_s.at[:, i * HALF : (i + 1) * HALF])
    at = rows_at(y * quarter, quarter)
    load(x_h.at[:, at], xr.at[:elecs])
    load(cot_h.at[:, at], cr.at[:elecs])
    loads[0].wait()
    loads[1].wait()
    halo_sems = halo_send.at[0], halo_recv.at[0]
    push(xv.at[:, patches - WIN :], halo, halo_sems, right)
    halo_copy = group(halo, halo_sems)
    go = {}

    def send_raw(c):
        here = slice(STARTS[c], STARTS[c] + CHUNKS[c])
        for k, (src, dst) in enumerate(((xv, xr), (cv, cr))):
            sems = go_send.at[c, k], go_recv.at[c, k]
            for d in (2, 1, 3):
                at = rows_at(lax.rem(y + d, 4) * quarter + STARTS[c], CHUNKS[c])
                push(src.at[:, at], dst.at[d * elecs : (d + 1) * elecs, here], sems, peer(y=d))
            go[c, k] = group(dst.at[elecs:, here], sems)

    send_raw(0)
    for copy in loads[2:]:
        copy.wait()

    bias0 = jnp.where(tm == 0, NEG, 0.0).astype(F32)

    def project_time(e, carry):
        q_t[e] = (mm(xv[e], w_t[:, :HALF], NN) * SCALE).astype(BF16)
        k_t[e, WIN:] = mm(xv[e], w_t[:, HALF : 2 * HALF], NN).astype(BF16)
        v_t[e, WIN:] = mm(xv[e], w_t[:, 2 * HALF :], NN).astype(BF16)
        g_t[e] = mm(cv[e], wo[HALF:, :], NT).astype(BF16)
        return carry

    lax.fori_loop(0, elecs, project_time, 0)

    def time_block(e, c, bias):
        rows, keys = slice(c * WIN, (c + 1) * WIN), slice(c * WIN, (c + 2) * WIN)
        att, dq, dk, dv = temporal_block(q_t[e, rows], g_t[e, rows], k_t[e, keys], v_t[e, keys], bias)
        att_t[e, rows] = att.astype(BF16)
        dq_t[e, rows] = dq.astype(BF16)
        return dk, dv

    def later_blocks(e, first_done):
        ones = time_block(e, 1, 0.0)
        twos = time_block(e, 2, 0.0)
        for ref, one, two in zip((dk_t, dv_t), ones, twos):
            if first_done:
                ref[e, :WIN] += one[:WIN]
            else:
                ref[e, :WIN] = one[:WIN]
            ref[e, WIN : 2 * WIN] = one[WIN:] + two[:WIN]
            ref[e, 2 * WIN :] = two[WIN:]

    def first_block(e, first_done):
        k_t[e, :WIN] = mm(halo[e], w_t[:, HALF : 2 * HALF], NN).astype(BF16)
        v_t[e, :WIN] = mm(halo[e], w_t[:, 2 * HALF :], NN).astype(BF16)
        for side, (ref, grad) in enumerate(zip((dk_t, dv_t), time_block(e, 0, bias0))):
            back_out[side, e] = grad[:WIN].astype(BF16)
            if first_done:
                ref[e, :WIN] = grad[WIN:]
            else:
                ref[e, :WIN] += grad[WIN:]

    def first_pair(i, carry):
        first_block(2 + 2 * i, True)
        first_block(3 + 2 * i, True)
        return carry

    def later_one(e, carry):
        later_blocks(e, True)
        return carry

    later_blocks(0, False)
    later_blocks(1, False)
    halo_copy.wait_recv()
    first_block(0, False)
    first_block(1, False)
    lax.fori_loop(0, elecs // 2 - 1, first_pair, 0)
    back_sems = halo_send.at[1], halo_recv.at[1]
    push(back_out, back_in, back_sems, left)
    back_copy = group(back_in, back_sems)
    lax.fori_loop(2, elecs, later_one, 0)
    send_raw(1)

    def span(c):
        return slice(STARTS[c], STARTS[c] + CHUNKS[c]), 4 * elecs * CHUNKS[c]

    def spatial_project(c):
        for k in range(2):
            go[c, k].wait_recv()
        here, rows = span(c)
        xi = xr[:, here].reshape(rows, width)
        shape = (4 * elecs, CHUNKS[c], HALF)
        q_s[:, : CHUNKS[c]] = (mm(xi, w_s[:, :HALF], NN) * SCALE).reshape(shape)
        k_s[:, : CHUNKS[c]] = mm(xi, w_s[:, HALF : 2 * HALF], NN).reshape(shape)
        v_s[:, : CHUNKS[c]] = mm(xi, w_s[:, 2 * HALF :], NN).reshape(shape)
        g_s[:, : CHUNKS[c]] = mm(cr[:, here].reshape(rows, width), wo[:HALF, :], NT).reshape(shape)

    def spatial_attend(c):
        def block(i, carry):
            for j in range(2):
                at = pl.ds(pl.multiple_of(i * 16 + j * 8, 8), 8)
                q, g, k, v = [ref[:, at, :].reshape(WIN, HALF).astype(BF16) for ref in (q_s, g_s, k_s, v_s)]
                for ref, value in zip((g_s, q_s, k_s, v_s), spatial_block(q, g, k, v)):
                    ref[:, at, :] = value.reshape(4 * elecs, 8, HALF)
            return carry

        lax.fori_loop(0, CHUNKS[c] // 16, block, 0)

    def spatial_end(c):
        here, rows = span(c)
        xi = xr[:, here].reshape(rows, width)
        grads = jnp.concatenate(
            [ref[:, : CHUNKS[c]].astype(BF16).reshape(rows, HALF) for ref in (q_s, k_s, v_s)], axis=1
        )
        dxs[:, here] = mm(grads, w_s[...], NT).astype(BF16).reshape(4 * elecs, CHUNKS[c], width)
        add_in = mm(xi, grads, TN)
        att = g_s[:, : CHUNKS[c]].astype(BF16).reshape(rows, HALF)
        add_out = mm(att, cr[:, here].reshape(rows, width), TN)
        if c == 0:
            acc_in_s[...] = add_in
            acc_out_s[...] = add_out
        else:
            acc_in_s[...] += add_in
            acc_out_s[...] += add_out

    returned = {}

    def send_back(c):
        here, _ = span(c)
        sems = ret_send.at[c], ret_recv.at[c]
        for d in (2, 1, 3):
            push(dxs.at[d * elecs : (d + 1) * elecs, here], dxr.at[d - 1, :, here], sems, peer(y=4 - d))
        returned[c] = group(dxr.at[:, :, here], sems)

    def place(c):
        here, _ = span(c)
        returned[c].wait_recv()
        for d in range(4):
            at = rows_at(lax.rem(y + d, 4) * quarter + STARTS[c], CHUNKS[c])
            if d == 0:
                piece = dxs[:elecs, here]
            else:
                piece = dxr[d - 1, :, here]
            out[:, at, :] = (dx_t[:, at, :] + piece.astype(F32)).astype(BF16)

    def summing(n):
        def exchange(p, step, axes, copies, whole):
            sems = ar_send.at[n, p, step], ar_recv.at[n, p, step]
            for i, by in others(axes):
                push(*copies(i, by), sems, peer(**by))
            return group(whole, sems)

        def own(axes, **by):
            at = [lax.rem(where[a] + by.get(a, 0), 2 if a == "core" else 4) for a in axes]
            return at[0] * (2 if axes[1] == "core" else 4) + at[1]

        waiting = [None, None]
        for p in range(2):
            axes = orders[p][0]
            waiting[p] = exchange(
                p,
                0,
                axes,
                lambda i, by: (ar_src.at[n, p, rows_at(own(axes, **by) * 256, 256)], recv_a.at[n, p, i - 1]),
                recv_a.at[n, p],
            )
        yield
        for p in range(2):
            waiting[p].wait_recv()
            total = ar_src[n, p, rows_at(own(orders[p][0]) * 256, 256)].astype(F32)
            for i in range(7):
                total = total + recv_a[n, p, i].astype(F32)
            part[n, p] = total.astype(BF16)
            axes = orders[p][1]
            waiting[p] = exchange(
                p,
                1,
                axes,
                lambda i, by: (part.at[n, p, rows_at(own(axes, **by) * 16, 16)], recv_b.at[n, p, i - 1]),
                recv_b.at[n, p],
            )
        yield
        for p in range(2):
            waiting[p].wait_recv()
            axes = orders[p][1]
            total = part[n, p, rows_at(own(axes) * 16, 16)].astype(F32)
            for i in range(15):
                total = total + recv_b[n, p, i].astype(F32)
            at = rows_at(own(orders[p][0]) * 256 + own(axes) * 16, 16)
            ar_out[n, p, at] = total.astype(BF16)
            spot = ar_out.at[n, p, at]
            waiting[p] = exchange(p, 2, axes, lambda i, by: (spot, spot), ar_out.at[n, p, :240])
        yield
        for p in range(2):
            waiting[p].wait_recv()
            axes = orders[p][0]
            spot = ar_out.at[n, p, rows_at(own(axes) * 256, 256)]
            waiting[p] = exchange(p, 3, axes, lambda i, by: (spot, spot), ar_out.at[n, p, :1792])
        yield
        for p in range(2):
            waiting[p].wait_recv()
            first = (1 - n) * HALF + p * 128
            for i in range(3):
                w_outs[i][:, first : first + 128] = ar_out[n, p, i * 512 : (i + 1) * 512]
            for i in range(2):
                low, column = (1 - n) * HALF, i * HALF + p * 128
                w_outs[3][low : low + HALF, column : column + 128] = ar_out[
                    n, p, 1536 + i * HALF : 1536 + (i + 1) * HALF
                ]
        yield

    back_copy.wait_recv()
    acc_in_t[...] = jnp.zeros_like(acc_in_t)
    acc_out_t[...] = jnp.zeros_like(acc_out_t)

    def end_time(e, carry):
        def full(own, side):
            tail = own[e, patches - WIN :] + back_in[side, e].astype(F32)
            return jnp.concatenate([own[e, : patches - WIN].astype(BF16), tail.astype(BF16)], axis=0)

        grads = jnp.concatenate([dq_t[e], full(dk_t, 0), full(dv_t, 1)], axis=1)
        dx_t[e] = mm(grads, w_t[...], NT)
        acc_in_t[...] += mm(xv[e], grads, TN)
        acc_out_t[...] += mm(att_t[e], cv[e], TN)
        return carry

    lax.fori_loop(0, elecs, end_time, 0)
    weight_rows(acc_in_t, acc_out_t, ar_src.at[0])
    time_sum, space_sum = summing(0), summing(1)
    next(time_sum)
    send_raw(2)
    spatial_project(0)
    spatial_attend(0)
    next(time_sum)
    spatial_end(0)
    spatial_project(1)
    spatial_attend(1)
    spatial_end(1)
    spatial_project(2)
    next(time_sum)
    send_back(0)
    spatial_attend(2)
    spatial_end(2)
    weight_rows(acc_in_s, acc_out_s, ar_src.at[1])
    next(space_sum)
    next(time_sum)
    send_back(2)
    next(space_sum)
    place(0)
    next(space_sum)
    send_back(1)
    next(time_sum)
    place(2)
    next(space_sum)
    place(1)
    next(space_sum)
    for whole in pending:
        whole.wait_send()


def end_kernel(dx, g0, g1, g2, g3, out, o0, o1, o2, o3):
    out[...] = dx[...]
    for grad, o in zip((g0, g1, g2, g3), (o0, o1, o2, o3)):
        o[...] = grad[...].astype(F32) * (1.0 / math.sqrt(196608))


def sds(shape, dtype):
    return jax.ShapeDtypeStruct(shape, dtype)


def shards(inputs, cotangent, w_query, w_key, w_value, w_out):
    _, elecs, patches, width = inputs.shape
    quarter = patches // 4
    vm, dma = pltpu.VMEM, pltpu.SemaphoreType.DMA
    tokens = (elecs, patches)
    ext = (elecs, patches + WIN)
    everyone = (4 * elecs, quarter)
    scratch = (
        [vm(tokens + (width,), BF16)] * 2
        + [vm((elecs, WIN, width), BF16)]
        + [vm((width, 3 * HALF), BF16)] * 2
        + [vm((width, width), BF16)]
        + [vm(tokens + (HALF,), BF16), vm(ext + (HALF,), BF16), vm(ext + (HALF,), BF16), vm(tokens + (HALF,), BF16)]
        + [vm(tokens + (HALF,), F32)] * 2
        + [vm(tokens + (HALF,), BF16)] * 2
        + [vm((2, elecs, WIN, HALF), BF16)] * 2
        + [vm(tokens + (width,), F32)]
        + [vm(everyone + (width,), BF16)] * 2
        + [vm((4 * elecs, CHUNKS[0], HALF), F32)] * 4
        + [vm(everyone + (width,), BF16), vm((3, elecs, quarter, width), BF16)]
        + [vm((width, 3 * HALF), F32), vm((HALF, width), F32)] * 2
        + [vm((2, 2, 2048, 128), BF16)]
        + [vm((2, 2, 7, 256, 128), BF16), vm((2, 2, 256, 128), BF16), vm((2, 2, 15, 16, 128), BF16)]
        + [vm((2, 2, 2048, 128), BF16)]
        + [dma((11,)), dma((2,)), dma((2,))]
        + [dma((3, 2))] * 2
        + [dma((3,))] * 2
        + [dma((2, 2, 4))] * 2
    )
    grad_inputs, *grads = pl.pallas_call(
        layer_kernel,
        out_shape=(sds(tokens + (width,), BF16),) + (sds((width, width), BF16),) * 4,
        in_specs=[pl.BlockSpec(memory_space=pl.ANY)] * 6,
        out_specs=(pl.BlockSpec(memory_space=pltpu.VMEM),) * 5,
        scratch_shapes=scratch,
        compiler_params=pltpu.CompilerParams(
            collective_id=0, has_side_effects=True, vmem_limit_bytes=VMEM_LIMIT
        ),
        cost_estimate=pl.CostEstimate(flops=2 * 10**10, bytes_accessed=10**7, transcendentals=2 * 10**6),
    )(inputs[0], cotangent[0], w_query, w_key, w_value, w_out)
    grad_inputs, *grads = pl.pallas_call(
        end_kernel,
        out_shape=(sds(tokens + (width,), BF16),) + (sds((width, width), F32),) * 4,
        in_specs=[pl.BlockSpec(memory_space=pltpu.VMEM)] * 5,
        out_specs=(pl.BlockSpec(memory_space=pltpu.VMEM),) * 5,
        compiler_params=pltpu.CompilerParams(vmem_limit_bytes=VMEM_LIMIT),
    )(grad_inputs, *grads)
    return (grad_inputs[None],) + tuple(grads)


def solution(mesh):
    return jax.shard_map(
        shards,
        mesh=mesh,
        in_specs=(P("dp", "elec", "tm", None), P("dp", "elec", "tm", None), P(), P(), P(), P()),
        out_specs=(P("dp", "elec", "tm", None), P(), P(), P(), P()),
        check_vma=False,
    )
```

time: 102 us -> 87.3 us (0.86)
  Pallas kernels: 95.2 us -> 86.6 us
  other arithmetic: 4.52 us -> 0 us
  local copies, waits for them, and re-layouts: 1.29 us -> 0 us
    pallas_call x1, Pallas kernels: 95.2 us -> 81.9 us  [shards(): pl.pallas_call(layer_kernel, out_shape=(sds(tokens + (width,), BF16),) +...]
    pallas_call x0 -> x1, Pallas kernels: none -> 4.7 us  [shards(): pl.pallas_call(end_kernel, out_shape=(sds(tokens + (width,), BF16),) + (s...]
    mul x2 -> x0, other arithmetic: 4.52 us -> none  [shards(): grad.astype(F32) * norm]
    unnamed x7 -> x0, local copies, waits for them, and re-layouts: 1.29 us -> none
where the time goes in v2:
time: 87.3 us; the launch traced here: 87.2 us
  Pallas kernels  86.6 us (99%)
    pallas_call x1, Pallas kernels, shards(): pl.pallas_call(layer_kernel, out_shape=(sds(tokens + (width,), BF16),) +...  81.9 us
    pallas_call x1, Pallas kernels, shards(): pl.pallas_call(end_kernel, out_shape=(sds(tokens + (width,), BF16),) + (s...  4.7 us

profile of v2, /device:TPU:1, one launch (start us, length us, event | category | flops | bytes accessed | tf_op | source)
XLA Modules:
  0.0 87.2 jit_solution(1436004381470815929)
XLA Ops:
  0.6 81.9 %shard_map.101 = (bf16[4,384,512]{2,1,0:T(8,128)(2,1)}, bf16[512,512]{1,0:T(8,128)(2,1)}, bf16[512,512]{1,0:T(8,128)(2,1)}, bf16[512,512]{1,0:T(8,128)(2,1)}, bf16[512,512]{1,0:T(8,128)(2,1)}) custom-call(bf16[4,384,512]{2,1,0:T(8,128)(2,1)} %bitcast.3, bf16[4,384,512]{2,1,0:T(8,128)(2,1)} %bitcast.4, bf16[512,512]{1,0:T(8,128)(2,1)} %wq_h.1, ...), custom_call_target="tpu_custom_call" | custom-call | flops 20000000000 | bytes 10000000 | tf_op jit(solution)/shard_map/pallas_call | solution.py:478
  82.5 4.7 %shard_map.102 = (bf16[4,384,512]{2,1,0:T(8,128)(2,1)}, f32[512,512]{1,0:T(8,128)}, f32[512,512]{1,0:T(8,128)}, f32[512,512]{1,0:T(8,128)}, f32[512,512]{1,0:T(8,128)}) custom-call(bf16[4,384,512]{2,1,0:T(8,128)(2,1)} %get-tuple-element.15.dx, bf16[512,512]{1,0:T(8,128)(2,1)} %get-tuple-element.16.g0, bf16[512,512]{1,0:T(8,128)(2,1)} %get-tuple-element.17.g1, ...), custom_call_target="tpu_custom_call" | custom-call | tf_op jit(solution)/shard_map/pallas_call | solution.py:489

commit v3 on v2

--- a/solution.py
+++ b/solution.py
@@ -28,60 +28,60 @@
 
 
 def stack_heads(rows):
-    head = lax.broadcasted_iota(jnp.int32, (1, HALF), 1) // HEAD
+    column = lax.broadcasted_iota(jnp.int32, (1, HALF), 1)
+    keeps = [(column >= h * HEAD) & (column < (h + 1) * HEAD) for h in range(HEADS)]
+    return jnp.concatenate([rows * keep.astype(F32).astype(BF16) for keep in keeps], axis=0)
+
+
+def pick_heads(rows):
+    r = rows.shape[0] // HEADS
+    even = lax.broadcasted_iota(jnp.int32, (r, 128), 1) < HEAD
     return jnp.concatenate(
-        [rows * (head == h).astype(F32).astype(BF16) for h in range(HEADS)], axis=0
+        [
+            jnp.where(even, rows[:r, :128], rows[r : 2 * r, :128]),
+            jnp.where(even, rows[2 * r : 3 * r, 128:], rows[3 * r :, 128:]),
+        ],
+        axis=1,
     )
 
 
-def pick_heads(rows):
-    count = rows.shape[0] // HEADS
-    head = lax.broadcasted_iota(jnp.int32, (count, HALF), 1) // HEAD
-    out = rows[:count]
-    for h in range(1, HEADS):
-        out = jnp.where(head == h, rows[h * count : (h + 1) * count], out)
-    return out
-
-
 def soft(scores, grad_probs):
-    peak = jnp.max(scores, axis=0, keepdims=True)
-    ex = jnp.exp(scores - peak)
-    probs = ex / jnp.sum(ex, axis=0, keepdims=True)
+    ex = jnp.exp(scores - jnp.max(scores, axis=0, keepdims=True))
+    probs = ex * (1.0 / jnp.sum(ex, axis=0, keepdims=True))
     delta = jnp.sum(probs * grad_probs, axis=0, keepdims=True)
-    return probs, probs * (grad_probs - delta)
-
-
-def temporal_block(q, ga, k, v, bias):
+    return probs.astype(BF16), (probs * (grad_probs - delta)).astype(BF16)
+
+
+def make_masks(older, older_low, newer_low, apart):
+    row = lax.broadcasted_iota(jnp.int32, (WIN, WIN), 0)
+    column = lax.broadcasted_iota(jnp.int32, (WIN, WIN), 1)
+    old = (row > column).astype(F32)
+    far = jnp.where(lax.rem(row, 8) == lax.rem(column, 8), 0.0, NEG).astype(F32)
+    for h in range(HEADS):
+        at = slice(h * WIN, (h + 1) * WIN)
+        older[:, at] = old
+        older_low[:, at] = old.astype(BF16)
+        newer_low[:, at] = (1.0 - old).astype(BF16)
+        apart[:, at] = far
+
+
+def temporal_block(q, ga, k, v, bias, older, older_low, newer_low):
     qs, gs = stack_heads(q), stack_heads(ga)
     st = mm(k, qs, NT)
     gt = mm(v, gs, NT)
-    shape = (WIN, HEADS * WIN)
-    older = lax.broadcasted_iota(jnp.int32, shape, 0) > lax.rem(
-        lax.broadcasted_iota(jnp.int32, shape, 1), WIN
-    )
-    probs, grad = soft(
-        jnp.where(older, st[:WIN] + bias, st[WIN:]), jnp.where(older, gt[:WIN], gt[WIN:])
-    )
-
-    def spread(t):
-        return jnp.concatenate(
-            [jnp.where(older, t, 0.0).astype(BF16), jnp.where(older, 0.0, t).astype(BF16)], axis=0
-        )
-
-    pt, dt = spread(probs), spread(grad)
+    old = older[...] > 0.5
+    early = st[:WIN] if bias is None else st[:WIN] + bias
+    probs, grad = soft(jnp.where(old, early, st[WIN:]), jnp.where(old, gt[:WIN], gt[WIN:]))
+    pt = jnp.concatenate([probs * older_low[...], probs * newer_low[...]], axis=0)
+    dt = jnp.concatenate([grad * older_low[...], grad * newer_low[...]], axis=0)
     att = pick_heads(mm(pt, v, TN))
     dq = pick_heads(mm(dt, k, TN)) * SCALE
     return att, dq, mm(dt, qs, NN), mm(pt, gs, NN)
 
 
-def spatial_block(q, ga, k, v):
+def spatial_block(q, ga, k, v, apart):
     qs, gs = stack_heads(q), stack_heads(ga)
-    shape = (WIN, HEADS * WIN)
-    same = lax.rem(lax.broadcasted_iota(jnp.int32, shape, 0), 8) == lax.rem(
-        lax.broadcasted_iota(jnp.int32, shape, 1), 8
-    )
-    probs, grad = soft(jnp.where(same, mm(k, qs, NT), NEG), mm(v, gs, NT))
-    pt, dt = probs.astype(BF16), grad.astype(BF16)
+    pt, dt = soft(mm(k, qs, NT) + apart[...], mm(v, gs, NT))
     att = pick_heads(mm(pt, v, TN))
     dq = pick_heads(mm(dt, k, TN)) * SCALE
     return att, dq, mm(dt, qs, NN), mm(pt, gs, NN)
@@ -117,7 +117,7 @@
     (
         xv, cv, halo, w_t, w_s, wo, q_t, k_t, v_t, g_t, dk_t, dv_t, att_t, dq_t, back_out, back_in, dx_t,
         xr, cr, q_s, k_s, v_s, g_s, dxs, dxr, acc_in_t, acc_out_t, acc_in_s, acc_out_s,
-        ar_src, recv_a, part, recv_b, ar_out,
+        ar_src, recv_a, part, recv_b, ar_out, older, older_low, newer_low, apart,
         load_sem, halo_send, halo_recv, go_send, go_recv, ret_send, ret_recv, ar_send, ar_recv,
     ) = rest[4:]
     elecs, patches, width = xv.shape
@@ -196,6 +196,8 @@
             go[c, k] = group(dst.at[elecs:, here], sems)
 
     send_raw(0)
+    masks = older, older_low, newer_low
+    make_masks(*masks, apart)
     for copy in loads[2:]:
         copy.wait()
 
@@ -212,14 +214,14 @@
 
     def time_block(e, c, bias):
         rows, keys = slice(c * WIN, (c + 1) * WIN), slice(c * WIN, (c + 2) * WIN)
-        att, dq, dk, dv = temporal_block(q_t[e, rows], g_t[e, rows], k_t[e, keys], v_t[e, keys], bias)
+        att, dq, dk, dv = temporal_block(q_t[e, rows], g_t[e, rows], k_t[e, keys], v_t[e, keys], bias, *masks)
         att_t[e, rows] = att.astype(BF16)
         dq_t[e, rows] = dq.astype(BF16)
         return dk, dv
 
     def later_blocks(e, first_done):
-        ones = time_block(e, 1, 0.0)
-        twos = time_block(e, 2, 0.0)
+        ones = time_block(e, 1, None)
+        twos = time_block(e, 2, None)
         for ref, one, two in zip((dk_t, dv_t), ones, twos):
             if first_done:
                 ref[e, :WIN] += one[:WIN]
@@ -278,7 +280,7 @@
             for j in range(2):
                 at = pl.ds(pl.multiple_of(i * 16 + j * 8, 8), 8)
                 q, g, k, v = [ref[:, at, :].reshape(WIN, HALF).astype(BF16) for ref in (q_s, g_s, k_s, v_s)]
-                for ref, value in zip((g_s, q_s, k_s, v_s), spatial_block(q, g, k, v)):
+                for ref, value in zip((g_s, q_s, k_s, v_s), spatial_block(q, g, k, v, apart)):
                     ref[:, at, :] = value.reshape(4 * elecs, 8, HALF)
             return carry
 
@@ -470,6 +472,7 @@
         + [vm((2, 2, 2048, 128), BF16)]
         + [vm((2, 2, 7, 256, 128), BF16), vm((2, 2, 256, 128), BF16), vm((2, 2, 15, 16, 128), BF16)]
         + [vm((2, 2, 2048, 128), BF16)]
+        + [vm((WIN, HEADS * WIN), t) for t in (F32, BF16, BF16, F32)]
         + [dma((11,)), dma((2,)), dma((2,))]
         + [dma((3, 2))] * 2
         + [dma((3,))] * 2
@@ -486,11 +489,14 @@
         ),
         cost_estimate=pl.CostEstimate(flops=2 * 10**10, bytes_accessed=10**7, transcendentals=2 * 10**6),
     )(inputs[0], cotangent[0], w_query, w_key, w_value, w_out)
+    token_spec = pl.BlockSpec((1, patches, width), lambda i: (i, 0, 0))
+    weight_spec = pl.BlockSpec((width // 4, width), lambda i: (i, 0))
     grad_inputs, *grads = pl.pallas_call(
         end_kernel,
+        grid=(4,),
         out_shape=(sds(tokens + (width,), BF16),) + (sds((width, width), F32),) * 4,
-        in_specs=[pl.BlockSpec(memory_space=pltpu.VMEM)] * 5,
-        out_specs=(pl.BlockSpec(memory_space=pltpu.VMEM),) * 5,
+        in_specs=[token_spec] + [weight_spec] * 4,
+        out_specs=(token_spec,) + (weight_spec,) * 4,
         compiler_params=pltpu.CompilerParams(vmem_limit_bytes=VMEM_LIMIT),
     )(grad_inputs, *grads)
     return (grad_inputs[None],) + tuple(grads)

time: 87.3 us -> 87.8 us (level)
  no operation moved by 1% of the time
where the time goes in v3:
time: 87.8 us; the launch traced here: 87.6 us
  Pallas kernels  86.9 us (99%)
    pallas_call x1, Pallas kernels, shards(): pl.pallas_call(layer_kernel, out_shape=(sds(tokens + (width,), BF16),) +...  81.9 us
    pallas_call x1, Pallas kernels, shards(): pl.pallas_call(end_kernel, grid=(4,), out_shape=(sds(tokens + (width,), B...  5.01 us

profile of v3, /device:TPU:1, one launch (start us, length us, event | category | flops | bytes accessed | tf_op | source)
XLA Modules:
  0.0 87.6 jit_solution(17285701052123337024)
XLA Ops:
  0.6 81.9 %shard_map.101 = (bf16[4,384,512]{2,1,0:T(8,128)(2,1)}, bf16[512,512]{1,0:T(8,128)(2,1)}, bf16[512,512]{1,0:T(8,128)(2,1)}, bf16[512,512]{1,0:T(8,128)(2,1)}, bf16[512,512]{1,0:T(8,128)(2,1)}) custom-call(bf16[4,384,512]{2,1,0:T(8,128)(2,1)} %bitcast.3, bf16[4,384,512]{2,1,0:T(8,128)(2,1)} %bitcast.4, bf16[512,512]{1,0:T(8,128)(2,1)} %wq_h.1, ...), custom_call_target="tpu_custom_call" | custom-call | flops 20000000000 | bytes 10000000 | tf_op jit(solution)/shard_map/pallas_call | solution.py:481
  82.5 5.0 %shard_map.102 = (bf16[4,384,512]{2,1,0:T(8,128)(2,1)}, f32[512,512]{1,0:T(8,128)}, f32[512,512]{1,0:T(8,128)}, f32[512,512]{1,0:T(8,128)}, f32[512,512]{1,0:T(8,128)}) custom-call(bf16[4,384,512]{2,1,0:T(8,128)(2,1)} %get-tuple-element.15.dx, bf16[512,512]{1,0:T(8,128)(2,1)} %get-tuple-element.16.g0, bf16[512,512]{1,0:T(8,128)(2,1)} %get-tuple-element.17.g1, ...), custom_call_target="tpu_custom_call" | custom-call | tf_op jit(solution)/shard_map/pallas_call | solution.py:494

commit v4 on v3

--- a/solution.py
+++ b/solution.py
@@ -117,7 +117,7 @@
     (
         xv, cv, halo, w_t, w_s, wo, q_t, k_t, v_t, g_t, dk_t, dv_t, att_t, dq_t, back_out, back_in, dx_t,
         xr, cr, q_s, k_s, v_s, g_s, dxs, dxr, acc_in_t, acc_out_t, acc_in_s, acc_out_s,
-        ar_src, recv_a, part, recv_b, ar_out, older, older_low, newer_low, apart,
+        ar_src, recv_c, part_c, recv_a, part, recv_b, ar_out, older, older_low, newer_low, apart,
         load_sem, halo_send, halo_recv, go_send, go_recv, ret_send, ret_recv, ar_send, ar_recv,
     ) = rest[4:]
     elecs, patches, width = xv.shape
@@ -132,35 +132,13 @@
         at = {n: lax.rem(where[n] + by.get(n, 0), 2 if n == "core" else 4) for n in where}
         return device_at(at["x"], at["y"], at["z"], at["core"])
 
-    orders = ((("x", "core"), ("z", "y")), (("z", "core"), ("x", "y")))
-
-    def others(axes):
-        low = 2 if axes[1] == "core" else 4
-        return [(i, {axes[0]: i // low, axes[1]: i % low}) for i in range(1, 4 * low)]
-
-    near = {tuple(sorted(by.items())) for axes in (orders[0] + orders[1]) for _, by in others(axes)}
-    near = sorted({tuple((n, v) for n, v in by if v) for by in near})
-    barrier = pltpu.get_barrier_semaphore()
-    for device in [right, left] + [peer(**dict(by)) for by in near]:
-        pl.semaphore_signal(barrier, inc=1, device_id=device, device_id_type=MESH)
-    pl.semaphore_wait(barrier, 2 + len(near))
-
-    pending = []
-
-    def push(src, dst, sems, device):
-        pltpu.make_async_remote_copy(
-            src_ref=src, dst_ref=dst, send_sem=sems[0], recv_sem=sems[1], device_id=device, device_id_type=MESH
-        ).start()
-
-    def group(ref, sems):
-        whole = pltpu.make_async_remote_copy(
-            src_ref=ref, dst_ref=ref, send_sem=sems[0], recv_sem=sems[1], device_id=right, device_id_type=MESH
-        )
-        pending.append(whole)
-        return whole
-
-    def rows_at(first, size):
-        return pl.ds(pl.multiple_of(first, 16), size)
+    orders = (("x", "z"), ("z", "x"))
+
+    def on_axis(a):
+        return [(d, {a: d}) for d in range(1, 4)]
+
+    def on_plane(b):
+        return [(i, {b: i // 4, "y": i % 4}) for i in range(1, 16)]
 
     loads = []
 
@@ -176,9 +154,34 @@
         load(w.at[:, HALF:], w_t.at[:, i * HALF : (i + 1) * HALF])
     for i, w in enumerate((wq_h, wk_h, wv_h)):
         load(w.at[:, :HALF], w_s.at[:, i * HALF : (i + 1) * HALF])
-    at = rows_at(y * quarter, quarter)
+    at = pl.ds(pl.multiple_of(y * quarter, 16), quarter)
     load(x_h.at[:, at], xr.at[:elecs])
     load(cot_h.at[:, at], cr.at[:elecs])
+
+    near = {tuple((n, v) for n, v in by.items() if v) for b in "xz" for _, by in on_plane(b)}
+    near = [(("core", 1),)] + sorted(near)
+    barrier = pltpu.get_barrier_semaphore()
+    for device in [right, left] + [peer(**dict(by)) for by in near]:
+        pl.semaphore_signal(barrier, inc=1, device_id=device, device_id_type=MESH)
+    pl.semaphore_wait(barrier, 2 + len(near))
+
+    pending = []
+
+    def push(src, dst, sems, device):
+        pltpu.make_async_remote_copy(
+            src_ref=src, dst_ref=dst, send_sem=sems[0], recv_sem=sems[1], device_id=device, device_id_type=MESH
+        ).start()
+
+    def group(ref, sems):
+        whole = pltpu.make_async_remote_copy(
+            src_ref=ref, dst_ref=ref, send_sem=sems[0], recv_sem=sems[1], device_id=right, device_id_type=MESH
+        )
+        pending.append(whole)
+        return whole
+
+    def rows_at(first, size):
+        return pl.ds(pl.multiple_of(first, 16), size)
+
     loads[0].wait()
     loads[1].wait()
     halo_sems = halo_send.at[0], halo_recv.at[0]
@@ -324,58 +327,62 @@
             out[:, at, :] = (dx_t[:, at, :] + piece.astype(F32)).astype(BF16)
 
     def summing(n):
-        def exchange(p, step, axes, copies, whole):
-            sems = ar_send.at[n, p, step], ar_recv.at[n, p, step]
-            for i, by in others(axes):
-                push(*copies(i, by), sems, peer(**by))
-            return group(whole, sems)
-
-        def own(axes, **by):
-            at = [lax.rem(where[a] + by.get(a, 0), 2 if a == "core" else 4) for a in axes]
-            return at[0] * (2 if axes[1] == "core" else 4) + at[1]
-
-        waiting = [None, None]
+        def sems(p, step):
+            return ar_send.at[n, p, step], ar_recv.at[n, p, step]
+
+        def spot_of(p, d=0):
+            return ar_out.at[n, p, rows_at(core * 1024 + lax.rem(where[orders[p][0]] + d, 4) * 256, 256)]
+
+        waiting, last = [None, None], [None, None]
         for p in range(2):
-            axes = orders[p][0]
-            waiting[p] = exchange(
-                p,
-                0,
-                axes,
-                lambda i, by: (ar_src.at[n, p, rows_at(own(axes, **by) * 256, 256)], recv_a.at[n, p, i - 1]),
-                recv_a.at[n, p],
-            )
+            push(ar_src.at[n, p, rows_at((1 - core) * 1024, 1024)], recv_c.at[n, p], sems(p, 0), peer(core=1))
+            waiting[p] = group(recv_c.at[n, p], sems(p, 0))
+        yield
+        for p, (a, b) in enumerate(orders):
+            waiting[p].wait_recv()
+            part_c[n, p] = (
+                ar_src[n, p, rows_at(core * 1024, 1024)].astype(F32) + recv_c[n, p].astype(F32)
+            ).astype(BF16)
+            for d, by in on_axis(a):
+                at = rows_at(lax.rem(where[a] + d, 4) * 256, 256)
+                push(part_c.at[n, p, at], recv_a.at[n, p, d - 1], sems(p, 1), peer(**by))
+            waiting[p] = group(recv_a.at[n, p], sems(p, 1))
+        yield
+        for p, (a, b) in enumerate(orders):
+            waiting[p].wait_recv()
+            total = part_c[n, p, rows_at(where[a] * 256, 256)].astype(F32)
+            for i in range(3):
+                total = total + recv_a[n, p, i].astype(F32)
+            part[n, p] = total.astype(BF16)
+            for i, by in on_plane(b):
+                at = rows_at((lax.rem(where[b] + by[b], 4) * 4 + lax.rem(y + by["y"], 4)) * 16, 16)
+                push(part.at[n, p, at], recv_b.at[n, p, i - 1], sems(p, 2), peer(**by))
+            waiting[p] = group(recv_b.at[n, p], sems(p, 2))
+        yield
+        for p, (a, b) in enumerate(orders):
+            waiting[p].wait_recv()
+            mine = (where[b] * 4 + y) * 16
+            total = part[n, p, rows_at(mine, 16)].astype(F32)
+            for i in range(15):
+                total = total + recv_b[n, p, i].astype(F32)
+            at = rows_at(core * 1024 + where[a] * 256 + mine, 16)
+            ar_out[n, p, at] = total.astype(BF16)
+            for _, by in on_plane(b):
+                push(ar_out.at[n, p, at], ar_out.at[n, p, at], sems(p, 3), peer(**by))
+            waiting[p] = group(ar_out.at[n, p, :240], sems(p, 3))
+        yield
+        for p, (a, b) in enumerate(orders):
+            waiting[p].wait_recv()
+            for _, by in on_axis(a):
+                push(spot_of(p), spot_of(p), sems(p, 4), peer(**by))
+            waiting[p] = group(ar_out.at[n, p, :768], sems(p, 4))
+            push(spot_of(p), spot_of(p), sems(p, 5), peer(core=1))
         yield
         for p in range(2):
             waiting[p].wait_recv()
-            total = ar_src[n, p, rows_at(own(orders[p][0]) * 256, 256)].astype(F32)
-            for i in range(7):
-                total = total + recv_a[n, p, i].astype(F32)
-            part[n, p] = total.astype(BF16)
-            axes = orders[p][1]
-            waiting[p] = exchange(
-                p,
-                1,
-                axes,
-                lambda i, by: (part.at[n, p, rows_at(own(axes, **by) * 16, 16)], recv_b.at[n, p, i - 1]),
-                recv_b.at[n, p],
-            )
-        yield
-        for p in range(2):
-            waiting[p].wait_recv()
-            axes = orders[p][1]
-            total = part[n, p, rows_at(own(axes) * 16, 16)].astype(F32)
-            for i in range(15):
-                total = total + recv_b[n, p, i].astype(F32)
-            at = rows_at(own(orders[p][0]) * 256 + own(axes) * 16, 16)
-            ar_out[n, p, at] = total.astype(BF16)
-            spot = ar_out.at[n, p, at]
-            waiting[p] = exchange(p, 2, axes, lambda i, by: (spot, spot), ar_out.at[n, p, :240])
-        yield
-        for p in range(2):
-            waiting[p].wait_recv()
-            axes = orders[p][0]
-            spot = ar_out.at[n, p, rows_at(own(axes) * 256, 256)]
-            waiting[p] = exchange(p, 3, axes, lambda i, by: (spot, spot), ar_out.at[n, p, :1792])
+            for d in range(1, 4):
+                push(spot_of(p, d), spot_of(p, d), sems(p, 5), peer(core=1))
+            waiting[p] = group(ar_out.at[n, p, :1024], sems(p, 5))
         yield
         for p in range(2):
             waiting[p].wait_recv()
@@ -408,12 +415,14 @@
     weight_rows(acc_in_t, acc_out_t, ar_src.at[0])
     time_sum, space_sum = summing(0), summing(1)
     next(time_sum)
+    spatial_project(0)
+    next(time_sum)
+    spatial_attend(0)
+    next(time_sum)
     send_raw(2)
-    spatial_project(0)
-    spatial_attend(0)
-    next(time_sum)
     spatial_end(0)
     spatial_project(1)
+    next(time_sum)
     spatial_attend(1)
     spatial_end(1)
     spatial_project(2)
@@ -424,13 +433,15 @@
     weight_rows(acc_in_s, acc_out_s, ar_src.at[1])
     next(space_sum)
     next(time_sum)
+    next(space_sum)
     send_back(2)
+    next(time_sum)
     next(space_sum)
     place(0)
     next(space_sum)
     send_back(1)
-    next(time_sum)
     place(2)
+    next(space_sum)
     next(space_sum)
     place(1)
     next(space_sum)
@@ -470,13 +481,14 @@
         + [vm(everyone + (width,), BF16), vm((3, elecs, quarter, width), BF16)]
         + [vm((width, 3 * HALF), F32), vm((HALF, width), F32)] * 2
         + [vm((2, 2, 2048, 128), BF16)]
-        + [vm((2, 2, 7, 256, 128), BF16), vm((2, 2, 256, 128), BF16), vm((2, 2, 15, 16, 128), BF16)]
+        + [vm((2, 2, 1024, 128), BF16)] * 2
+        + [vm((2, 2, 3, 256, 128), BF16), vm((2, 2, 256, 128), BF16), vm((2, 2, 15, 16, 128), BF16)]
         + [vm((2, 2, 2048, 128), BF16)]
         + [vm((WIN, HEADS * WIN), t) for t in (F32, BF16, BF16, F32)]
         + [dma((11,)), dma((2,)), dma((2,))]
         + [dma((3, 2))] * 2
         + [dma((3,))] * 2
-        + [dma((2, 2, 4))] * 2
+        + [dma((2, 2, 6))] * 2
     )
     grad_inputs, *grads = pl.pallas_call(
         layer_kernel,
@@ -489,14 +501,11 @@
         ),
         cost_estimate=pl.CostEstimate(flops=2 * 10**10, bytes_accessed=10**7, transcendentals=2 * 10**6),
     )(inputs[0], cotangent[0], w_query, w_key, w_value, w_out)
-    token_spec = pl.BlockSpec((1, patches, width), lambda i: (i, 0, 0))
-    weight_spec = pl.BlockSpec((width // 4, width), lambda i: (i, 0))
     grad_inputs, *grads = pl.pallas_call(
         end_kernel,
-        grid=(4,),
         out_shape=(sds(tokens + (width,), BF16),) + (sds((width, width), F32),) * 4,
-        in_specs=[token_spec] + [weight_spec] * 4,
-        out_specs=(token_spec,) + (weight_spec,) * 4,
+        in_specs=[pl.BlockSpec(memory_space=pltpu.VMEM)] * 5,
+        out_specs=(pl.BlockSpec(memory_space=pltpu.VMEM),) * 5,
         compiler_params=pltpu.CompilerParams(vmem_limit_bytes=VMEM_LIMIT),
     )(grad_inputs, *grads)
     return (grad_inputs[None],) + tuple(grads)

time: 87.8 us -> 87.9 us (level)
  no operation moved by 1% of the time
where the time goes in v4:
time: 87.9 us; the launch traced here: 87.8 us
  Pallas kernels  87.1 us (99%)
    pallas_call x1, Pallas kernels, shards(): pl.pallas_call(layer_kernel, out_shape=(sds(tokens + (width,), BF16),) +...  82.4 us
    pallas_call x1, Pallas kernels, shards(): pl.pallas_call(end_kernel, out_shape=(sds(tokens + (width,), BF16),) + (s...  4.7 us

profile of v4, /device:TPU:1, one launch (start us, length us, event | category | flops | bytes accessed | tf_op | source)
XLA Modules:
  0.0 87.8 jit_solution(2022071292342874771)
XLA Ops:
  0.6 82.4 %shard_map.101 = (bf16[4,384,512]{2,1,0:T(8,128)(2,1)}, bf16[512,512]{1,0:T(8,128)(2,1)}, bf16[512,512]{1,0:T(8,128)(2,1)}, bf16[512,512]{1,0:T(8,128)(2,1)}, bf16[512,512]{1,0:T(8,128)(2,1)}) custom-call(bf16[4,384,512]{2,1,0:T(8,128)(2,1)} %bitcast.3, bf16[4,384,512]{2,1,0:T(8,128)(2,1)} %bitcast.4, bf16[512,512]{1,0:T(8,128)(2,1)} %wq_h.1, ...), custom_call_target="tpu_custom_call" | custom-call | flops 20000000000 | bytes 10000000 | tf_op jit(solution)/shard_map/pallas_call | solution.py:493
  83.1 4.7 %shard_map.102 = (bf16[4,384,512]{2,1,0:T(8,128)(2,1)}, f32[512,512]{1,0:T(8,128)}, f32[512,512]{1,0:T(8,128)}, f32[512,512]{1,0:T(8,128)}, f32[512,512]{1,0:T(8,128)}) custom-call(bf16[4,384,512]{2,1,0:T(8,128)(2,1)} %get-tuple-element.15.dx, bf16[512,512]{1,0:T(8,128)(2,1)} %get-tuple-element.16.g0, bf16[512,512]{1,0:T(8,128)(2,1)} %get-tuple-element.17.g1, ...), custom_call_target="tpu_custom_call" | custom-call | tf_op jit(solution)/shard_map/pallas_call | solution.py:504

commit v5 on v4

--- a/solution.py
+++ b/solution.py
@@ -117,8 +117,8 @@
     (
         xv, cv, halo, w_t, w_s, wo, q_t, k_t, v_t, g_t, dk_t, dv_t, att_t, dq_t, back_out, back_in, dx_t,
         xr, cr, q_s, k_s, v_s, g_s, dxs, dxr, acc_in_t, acc_out_t, acc_in_s, acc_out_s,
-        ar_src, recv_c, part_c, recv_a, part, recv_b, ar_out, older, older_low, newer_low, apart,
-        load_sem, halo_send, halo_recv, go_send, go_recv, ret_send, ret_recv, ar_send, ar_recv,
+        ar_src, recv_c, part_c, recv_a, part, recv_b, ar_out, older, older_low, newer_low, apart, via, via_back,
+        load_sem, halo_send, halo_recv, go_send, go_recv, ret_send, ret_recv, ar_send, ar_recv, via_send, via_recv,
     ) = rest[4:]
     elecs, patches, width = xv.shape
     quarter = patches // 4
@@ -189,14 +189,31 @@
     halo_copy = group(halo, halo_sems)
     go = {}
 
+    ways = (1, 3)
+    hops = {}
+
     def send_raw(c):
         here = slice(STARTS[c], STARTS[c] + CHUNKS[c])
+
+        def part(src, d):
+            return src.at[:, rows_at(lax.rem(y + d, 4) * quarter + STARTS[c], CHUNKS[c])]
+
+        for k, src in enumerate((xv, cv)):
+            sems = via_send.at[0, c, k], via_recv.at[0, c, k]
+            push(part(src, 2), via.at[k, :, here], sems, peer(y=ways[k]))
+            hops[c, k] = group(via.at[k, :, here], sems)
         for k, (src, dst) in enumerate(((xv, xr), (cv, cr))):
             sems = go_send.at[c, k], go_recv.at[c, k]
-            for d in (2, 1, 3):
-                at = rows_at(lax.rem(y + d, 4) * quarter + STARTS[c], CHUNKS[c])
-                push(src.at[:, at], dst.at[d * elecs : (d + 1) * elecs, here], sems, peer(y=d))
+            for d in (1, 3):
+                push(part(src, d), dst.at[d * elecs : (d + 1) * elecs, here], sems, peer(y=d))
             go[c, k] = group(dst.at[elecs:, here], sems)
+
+    def pass_raw(c):
+        here = slice(STARTS[c], STARTS[c] + CHUNKS[c])
+        for k, dst in enumerate((xr, cr)):
+            hops[c, k].wait_recv()
+            sems = go_send.at[c, k], go_recv.at[c, k]
+            push(via.at[k, :, here], dst.at[2 * elecs : 3 * elecs, here], sems, peer(y=ways[k]))
 
     send_raw(0)
     masks = older, older_low, newer_low
@@ -255,6 +272,7 @@
     later_blocks(0, False)
     later_blocks(1, False)
     halo_copy.wait_recv()
+    pass_raw(0)
     first_block(0, False)
     first_block(1, False)
     lax.fori_loop(0, elecs // 2 - 1, first_pair, 0)
@@ -306,14 +324,27 @@
             acc_in_s[...] += add_in
             acc_out_s[...] += add_out
 
-    returned = {}
+    returned, hops_back = {}, {}
 
     def send_back(c):
         here, _ = span(c)
+        for k in range(2):
+            first = 2 * elecs + k * (elecs // 2)
+            sems = via_send.at[1, c, k], via_recv.at[1, c, k]
+            push(dxs.at[first : first + elecs // 2, here], via_back.at[k, :, here], sems, peer(y=ways[k]))
+            hops_back[c, k] = group(via_back.at[k, :, here], sems)
         sems = ret_send.at[c], ret_recv.at[c]
-        for d in (2, 1, 3):
+        for d in (1, 3):
             push(dxs.at[d * elecs : (d + 1) * elecs, here], dxr.at[d - 1, :, here], sems, peer(y=4 - d))
         returned[c] = group(dxr.at[:, :, here], sems)
+
+    def pass_back(c):
+        here, _ = span(c)
+        for k in range(2):
+            hops_back[c, k].wait_recv()
+            half = slice(k * (elecs // 2), (k + 1) * (elecs // 2))
+            sems = ret_send.at[c], ret_recv.at[c]
+            push(via_back.at[k, :, here], dxr.at[1, half, here], sems, peer(y=ways[k]))
 
     def place(c):
         here, _ = span(c)
@@ -417,11 +448,13 @@
     next(time_sum)
     spatial_project(0)
     next(time_sum)
+    pass_raw(1)
     spatial_attend(0)
     next(time_sum)
     send_raw(2)
     spatial_end(0)
     spatial_project(1)
+    pass_raw(2)
     next(time_sum)
     spatial_attend(1)
     spatial_end(1)
@@ -432,16 +465,19 @@
     spatial_end(2)
     weight_rows(acc_in_s, acc_out_s, ar_src.at[1])
     next(space_sum)
-    next(time_sum)
-    next(space_sum)
+    pass_back(0)
+    next(time_sum)
     send_back(2)
-    next(time_sum)
+    next(space_sum)
+    next(time_sum)
+    pass_back(2)
     next(space_sum)
     place(0)
     next(space_sum)
     send_back(1)
     place(2)
     next(space_sum)
+    pass_back(1)
     next(space_sum)
     place(1)
     next(space_sum)
@@ -485,10 +521,12 @@
         + [vm((2, 2, 3, 256, 128), BF16), vm((2, 2, 256, 128), BF16), vm((2, 2, 15, 16, 128), BF16)]
         + [vm((2, 2, 2048, 128), BF16)]
         + [vm((WIN, HEADS * WIN), t) for t in (F32, BF16, BF16, F32)]
+        + [vm((2, elecs, quarter, width), BF16), vm((2, elecs // 2, quarter, width), BF16)]
         + [dma((11,)), dma((2,)), dma((2,))]
         + [dma((3, 2))] * 2
         + [dma((3,))] * 2
         + [dma((2, 2, 6))] * 2
+        + [dma((2, 3, 2))] * 2
     )
     grad_inputs, *grads = pl.pallas_call(
         layer_kernel,

time: 87.9 us -> 90.5 us (1.030)
  Pallas kernels: 87.1 us -> 89.7 us
    pallas_call x1, Pallas kernels: 82.4 us -> 85 us  [shards(): pl.pallas_call(layer_kernel, out_shape=(sds(tokens + (width,), BF16),) +...]
where the time goes in v5:
time: 90.5 us; the launch traced here: 90.3 us
  Pallas kernels  89.7 us (99%)
    pallas_call x1, Pallas kernels, shards(): pl.pallas_call(layer_kernel, out_shape=(sds(tokens + (width,), BF16),) +...  85 us
    pallas_call x1, Pallas kernels, shards(): pl.pallas_call(end_kernel, out_shape=(sds(tokens + (width,), BF16),) + (s...  4.7 us

profile of v5, /device:TPU:1, one launch (start us, length us, event | category | flops | bytes accessed | tf_op | source)
XLA Modules:
  0.0 90.3 jit_solution(2483479467558487507)
XLA Ops:
  0.6 85.0 %shard_map.101 = (bf16[4,384,512]{2,1,0:T(8,128)(2,1)}, bf16[512,512]{1,0:T(8,128)(2,1)}, bf16[512,512]{1,0:T(8,128)(2,1)}, bf16[512,512]{1,0:T(8,128)(2,1)}, bf16[512,512]{1,0:T(8,128)(2,1)}) custom-call(bf16[4,384,512]{2,1,0:T(8,128)(2,1)} %bitcast.3, bf16[4,384,512]{2,1,0:T(8,128)(2,1)} %bitcast.4, bf16[512,512]{1,0:T(8,128)(2,1)} %wq_h.1, ...), custom_call_target="tpu_custom_call" | custom-call | flops 20000000000 | bytes 10000000 | tf_op jit(solution)/shard_map/pallas_call | solution.py:531
  85.6 4.7 %shard_map.102 = (bf16[4,384,512]{2,1,0:T(8,128)(2,1)}, f32[512,512]{1,0:T(8,128)}, f32[512,512]{1,0:T(8,128)}, f32[512,512]{1,0:T(8,128)}, f32[512,512]{1,0:T(8,128)}) custom-call(bf16[4,384,512]{2,1,0:T(8,128)(2,1)} %get-tuple-element.15.dx, bf16[512,512]{1,0:T(8,128)(2,1)} %get-tuple-element.16.g0, bf16[512,512]{1,0:T(8,128)(2,1)} %get-tuple-element.17.g1, ...), custom_call_target="tpu_custom_call" | custom-call | tf_op jit(solution)/shard_map/pallas_call | solution.py:542

commit v6 on v4

--- a/solution.py
+++ b/solution.py
@@ -65,7 +65,13 @@
         apart[:, at] = far
 
 
-def temporal_block(q, ga, k, v, bias, older, older_low, newer_low):
+def diagonal(cols):
+    return jnp.concatenate(
+        [cols[h * HEAD : (h + 1) * HEAD, h * WIN : (h + 1) * WIN] for h in range(HEADS)], axis=0
+    )
+
+
+def temporal_block(q, ga, k, v, k_cols, v_cols, bias, older, older_low, newer_low):
     qs, gs = stack_heads(q), stack_heads(ga)
     st = mm(k, qs, NT)
     gt = mm(v, gs, NT)
@@ -74,9 +80,9 @@
     probs, grad = soft(jnp.where(old, early, st[WIN:]), jnp.where(old, gt[:WIN], gt[WIN:]))
     pt = jnp.concatenate([probs * older_low[...], probs * newer_low[...]], axis=0)
     dt = jnp.concatenate([grad * older_low[...], grad * newer_low[...]], axis=0)
-    att = pick_heads(mm(pt, v, TN))
-    dq = pick_heads(mm(dt, k, TN)) * SCALE
-    return att, dq, mm(dt, qs, NN), mm(pt, gs, NN)
+    att = diagonal(mm(v_cols, pt, NN)).astype(BF16)
+    dq = (diagonal(mm(k_cols, dt, NN)) * SCALE).astype(BF16)
+    return att, dq.T, mm(dt, qs, NN), mm(pt, gs, NN)
 
 
 def spatial_block(q, ga, k, v, apart):
@@ -115,7 +121,7 @@
 def layer_kernel(x_h, cot_h, wq_h, wk_h, wv_h, wo_h, out, *rest):
     w_outs = rest[:4]
     (
-        xv, cv, halo, w_t, w_s, wo, q_t, k_t, v_t, g_t, dk_t, dv_t, att_t, dq_t, back_out, back_in, dx_t,
+        xv, cv, halo, w_t, w_s, wo, q_t, k_t, v_t, g_t, dk_t, dv_t, att_t, dq_t, kc_t, vc_t, back_out, back_in, dx_t,
         xr, cr, q_s, k_s, v_s, g_s, dxs, dxr, acc_in_t, acc_out_t, acc_in_s, acc_out_s,
         ar_src, recv_c, part_c, recv_a, part, recv_b, ar_out, older, older_low, newer_low, apart,
         load_sem, halo_send, halo_recv, go_send, go_recv, ret_send, ret_recv, ar_send, ar_recv,
@@ -208,8 +214,10 @@
 
     def project_time(e, carry):
         q_t[e] = (mm(xv[e], w_t[:, :HALF], NN) * SCALE).astype(BF16)
-        k_t[e, WIN:] = mm(xv[e], w_t[:, HALF : 2 * HALF], NN).astype(BF16)
-        v_t[e, WIN:] = mm(xv[e], w_t[:, 2 * HALF :], NN).astype(BF16)
+        for own, cols, i in ((k_t, kc_t, 1), (v_t, vc_t, 2)):
+            t = mm(xv[e], w_t[:, i * HALF : (i + 1) * HALF], NN).astype(BF16)
+            own[e, WIN:] = t
+            cols[e, :, WIN:] = t.T
         g_t[e] = mm(cv[e], wo[HALF:, :], NT).astype(BF16)
         return carry
 
@@ -217,9 +225,11 @@
 
     def time_block(e, c, bias):
         rows, keys = slice(c * WIN, (c + 1) * WIN), slice(c * WIN, (c + 2) * WIN)
-        att, dq, dk, dv = temporal_block(q_t[e, rows], g_t[e, rows], k_t[e, keys], v_t[e, keys], bias, *masks)
-        att_t[e, rows] = att.astype(BF16)
-        dq_t[e, rows] = dq.astype(BF16)
+        att, dq, dk, dv = temporal_block(
+            q_t[e, rows], g_t[e, rows], k_t[e, keys], v_t[e, keys], kc_t[e, :, keys], vc_t[e, :, keys], bias, *masks
+        )
+        att_t[e, :, rows] = att
+        dq_t[e, rows] = dq
         return dk, dv
 
     def later_blocks(e, first_done):
@@ -234,8 +244,10 @@
             ref[e, 2 * WIN :] = two[WIN:]
 
     def first_block(e, first_done):
-        k_t[e, :WIN] = mm(halo[e], w_t[:, HALF : 2 * HALF], NN).astype(BF16)
-        v_t[e, :WIN] = mm(halo[e], w_t[:, 2 * HALF :], NN).astype(BF16)
+        for own, cols, i in ((k_t, kc_t, 1), (v_t, vc_t, 2)):
+            t = mm(halo[e], w_t[:, i * HALF : (i + 1) * HALF], NN).astype(BF16)
+            own[e, :WIN] = t
+            cols[e, :, :WIN] = t.T
         for side, (ref, grad) in enumerate(zip((dk_t, dv_t), time_block(e, 0, bias0))):
             back_out[side, e] = grad[:WIN].astype(BF16)
             if first_done:
@@ -308,16 +320,17 @@
 
     returned = {}
 
-    def send_back(c):
+    def send_back(c, steps):
         here, _ = span(c)
-        sems = ret_send.at[c], ret_recv.at[c]
-        for d in (2, 1, 3):
+        sems = ret_send.at[c, steps[0] % 2], ret_recv.at[c, steps[0] % 2]
+        for d in steps:
             push(dxs.at[d * elecs : (d + 1) * elecs, here], dxr.at[d - 1, :, here], sems, peer(y=4 - d))
-        returned[c] = group(dxr.at[:, :, here], sems)
+        returned[c, steps[0] % 2] = group(dxr.at[: len(steps), :, here], sems)
 
     def place(c):
         here, _ = span(c)
-        returned[c].wait_recv()
+        for i in range(2):
+            returned[c, i].wait_recv()
         for d in range(4):
             at = rows_at(lax.rem(y + d, 4) * quarter + STARTS[c], CHUNKS[c])
             if d == 0:
@@ -408,7 +421,7 @@
         grads = jnp.concatenate([dq_t[e], full(dk_t, 0), full(dv_t, 1)], axis=1)
         dx_t[e] = mm(grads, w_t[...], NT)
         acc_in_t[...] += mm(xv[e], grads, TN)
-        acc_out_t[...] += mm(att_t[e], cv[e], TN)
+        acc_out_t[...] += mm(att_t[e], cv[e], NN)
         return carry
 
     lax.fori_loop(0, elecs, end_time, 0)
@@ -423,27 +436,30 @@
     spatial_end(0)
     spatial_project(1)
     next(time_sum)
+    send_back(0, (2,))
+    send_back(0, (1, 3))
     spatial_attend(1)
     spatial_end(1)
     spatial_project(2)
     next(time_sum)
-    send_back(0)
     spatial_attend(2)
     spatial_end(2)
     weight_rows(acc_in_s, acc_out_s, ar_src.at[1])
     next(space_sum)
     next(time_sum)
     next(space_sum)
-    send_back(2)
-    next(time_sum)
-    next(space_sum)
+    next(time_sum)
+    next(space_sum)
+    send_back(1, (1, 3))
     place(0)
     next(space_sum)
-    send_back(1)
+    send_back(1, (2,))
+    send_back(2, (2,))
+    send_back(2, (1, 3))
+    next(space_sum)
+    next(space_sum)
+    place(1)
     place(2)
-    next(space_sum)
-    next(space_sum)
-    place(1)
     next(space_sum)
     for whole in pending:
         whole.wait_send()
@@ -473,7 +489,8 @@
         + [vm((width, width), BF16)]
         + [vm(tokens + (HALF,), BF16), vm(ext + (HALF,), BF16), vm(ext + (HALF,), BF16), vm(tokens + (HALF,), BF16)]
         + [vm(tokens + (HALF,), F32)] * 2
-        + [vm(tokens + (HALF,), BF16)] * 2
+        + [vm((elecs, HALF, patches), BF16), vm(tokens + (HALF,), BF16)]
+        + [vm((elecs, HALF, patches + WIN), BF16)] * 2
         + [vm((2, elecs, WIN, HALF), BF16)] * 2
         + [vm(tokens + (width,), F32)]
         + [vm(everyone + (width,), BF16)] * 2
@@ -487,7 +504,7 @@
         + [vm((WIN, HEADS * WIN), t) for t in (F32, BF16, BF16, F32)]
         + [dma((11,)), dma((2,)), dma((2,))]
         + [dma((3, 2))] * 2
-        + [dma((3,))] * 2
+        + [dma((3, 2))] * 2
         + [dma((2, 2, 6))] * 2
     )
     grad_inputs, *grads = pl.pallas_call(

time: 87.9 us -> 93 us (1.058)
  Pallas kernels: 87.1 us -> 92.2 us
    pallas_call x1, Pallas kernels: 82.4 us -> 87.5 us  [shards(): pl.pallas_call(layer_kernel, out_shape=(sds(tokens + (width,), BF16),) +...]
where the time goes in v6:
time: 93 us; the launch traced here: 92.8 us
  Pallas kernels  92.2 us (99%)
    pallas_call x1, Pallas kernels, shards(): pl.pallas_call(layer_kernel, out_shape=(sds(tokens + (width,), BF16),) +...  87.5 us
    pallas_call x1, Pallas kernels, shards(): pl.pallas_call(end_kernel, out_shape=(sds(tokens + (width,), BF16),) + (s...  4.7 us

profile of v6, /device:TPU:1, one launch (start us, length us, event | category | flops | bytes accessed | tf_op | source)
XLA Modules:
  0.0 92.8 jit_solution(4524095568419901656)
XLA Ops:
  0.6 87.5 %shard_map.101 = (bf16[4,384,512]{2,1,0:T(8,128)(2,1)}, bf16[512,512]{1,0:T(8,128)(2,1)}, bf16[512,512]{1,0:T(8,128)(2,1)}, bf16[512,512]{1,0:T(8,128)(2,1)}, bf16[512,512]{1,0:T(8,128)(2,1)}) custom-call(bf16[4,384,512]{2,1,0:T(8,128)(2,1)} %bitcast.3, bf16[4,384,512]{2,1,0:T(8,128)(2,1)} %bitcast.4, bf16[512,512]{1,0:T(8,128)(2,1)} %wq_h.1, ...), custom_call_target="tpu_custom_call" | custom-call | flops 20000000000 | bytes 10000000 | tf_op jit(solution)/shard_map/pallas_call | solution.py:510
  88.1 4.7 %shard_map.102 = (bf16[4,384,512]{2,1,0:T(8,128)(2,1)}, f32[512,512]{1,0:T(8,128)}, f32[512,512]{1,0:T(8,128)}, f32[512,512]{1,0:T(8,128)}, f32[512,512]{1,0:T(8,128)}) custom-call(bf16[4,384,512]{2,1,0:T(8,128)(2,1)} %get-tuple-element.15.dx, bf16[512,512]{1,0:T(8,128)(2,1)} %get-tuple-element.16.g0, bf16[512,512]{1,0:T(8,128)(2,1)} %get-tuple-element.17.g1, ...), custom_call_target="tpu_custom_call" | custom-call | tf_op jit(solution)/shard_map/pallas_call | solution.py:521

commit v7 on v6

--- a/solution.py
+++ b/solution.py
@@ -124,7 +124,7 @@
         xv, cv, halo, w_t, w_s, wo, q_t, k_t, v_t, g_t, dk_t, dv_t, att_t, dq_t, kc_t, vc_t, back_out, back_in, dx_t,
         xr, cr, q_s, k_s, v_s, g_s, dxs, dxr, acc_in_t, acc_out_t, acc_in_s, acc_out_s,
         ar_src, recv_c, part_c, recv_a, part, recv_b, ar_out, older, older_low, newer_low, apart,
-        load_sem, halo_send, halo_recv, go_send, go_recv, ret_send, ret_recv, ar_send, ar_recv,
+        load_sem, halo_send, halo_recv, go_send, go_recv, ret_send, ret_recv, ar_send, ar_recv, all_send, all_recv,
     ) = rest[4:]
     elecs, patches, width = xv.shape
     quarter = patches // 4
@@ -339,74 +339,83 @@
                 piece = dxr[d - 1, :, here]
             out[:, at, :] = (dx_t[:, at, :] + piece.astype(F32)).astype(BF16)
 
-    def summing(n):
+    waiting = {}
+
+    def gather(n):
         def sems(p, step):
             return ar_send.at[n, p, step], ar_recv.at[n, p, step]
 
-        def spot_of(p, d=0):
-            return ar_out.at[n, p, rows_at(core * 1024 + lax.rem(where[orders[p][0]] + d, 4) * 256, 256)]
-
-        waiting, last = [None, None], [None, None]
         for p in range(2):
             push(ar_src.at[n, p, rows_at((1 - core) * 1024, 1024)], recv_c.at[n, p], sems(p, 0), peer(core=1))
-            waiting[p] = group(recv_c.at[n, p], sems(p, 0))
+            waiting[n, p] = group(recv_c.at[n, p], sems(p, 0))
         yield
         for p, (a, b) in enumerate(orders):
-            waiting[p].wait_recv()
+            waiting[n, p].wait_recv()
             part_c[n, p] = (
                 ar_src[n, p, rows_at(core * 1024, 1024)].astype(F32) + recv_c[n, p].astype(F32)
             ).astype(BF16)
             for d, by in on_axis(a):
                 at = rows_at(lax.rem(where[a] + d, 4) * 256, 256)
                 push(part_c.at[n, p, at], recv_a.at[n, p, d - 1], sems(p, 1), peer(**by))
-            waiting[p] = group(recv_a.at[n, p], sems(p, 1))
-        yield
+            waiting[n, p] = group(recv_a.at[n, p], sems(p, 1))
+        yield
+
+    def finish():
+        def sems(p, step):
+            return all_send.at[p, step], all_recv.at[p, step]
+
+        def spot_of(p, d=0):
+            return ar_out.at[p, :, rows_at(core * 1024 + lax.rem(where[orders[p][0]] + d, 4) * 256, 256)]
+
         for p, (a, b) in enumerate(orders):
-            waiting[p].wait_recv()
-            total = part_c[n, p, rows_at(where[a] * 256, 256)].astype(F32)
-            for i in range(3):
-                total = total + recv_a[n, p, i].astype(F32)
-            part[n, p] = total.astype(BF16)
+            for n in range(2):
+                waiting[n, p].wait_recv()
+                total = part_c[n, p, rows_at(where[a] * 256, 256)].astype(F32)
+                for i in range(3):
+                    total = total + recv_a[n, p, i].astype(F32)
+                part[p, n] = total.astype(BF16)
             for i, by in on_plane(b):
                 at = rows_at((lax.rem(where[b] + by[b], 4) * 4 + lax.rem(y + by["y"], 4)) * 16, 16)
-                push(part.at[n, p, at], recv_b.at[n, p, i - 1], sems(p, 2), peer(**by))
-            waiting[p] = group(recv_b.at[n, p], sems(p, 2))
+                push(part.at[p, :, at], recv_b.at[p, i - 1], sems(p, 0), peer(**by))
+            waiting[p] = group(recv_b.at[p], sems(p, 0))
         yield
         for p, (a, b) in enumerate(orders):
             waiting[p].wait_recv()
             mine = (where[b] * 4 + y) * 16
-            total = part[n, p, rows_at(mine, 16)].astype(F32)
+            total = part[p, :, rows_at(mine, 16)].astype(F32)
             for i in range(15):
-                total = total + recv_b[n, p, i].astype(F32)
+                total = total + recv_b[p, i].astype(F32)
             at = rows_at(core * 1024 + where[a] * 256 + mine, 16)
-            ar_out[n, p, at] = total.astype(BF16)
+            ar_out[p, :, at] = total.astype(BF16)
             for _, by in on_plane(b):
-                push(ar_out.at[n, p, at], ar_out.at[n, p, at], sems(p, 3), peer(**by))
-            waiting[p] = group(ar_out.at[n, p, :240], sems(p, 3))
+                push(ar_out.at[p, :, at], ar_out.at[p, :, at], sems(p, 1), peer(**by))
+            waiting[p] = group(ar_out.at[p, :, :240], sems(p, 1))
         yield
         for p, (a, b) in enumerate(orders):
             waiting[p].wait_recv()
             for _, by in on_axis(a):
-                push(spot_of(p), spot_of(p), sems(p, 4), peer(**by))
-            waiting[p] = group(ar_out.at[n, p, :768], sems(p, 4))
-            push(spot_of(p), spot_of(p), sems(p, 5), peer(core=1))
+                push(spot_of(p), spot_of(p), sems(p, 2), peer(**by))
+            waiting[p] = group(ar_out.at[p, :, :768], sems(p, 2))
+            push(spot_of(p), spot_of(p), sems(p, 3), peer(core=1))
         yield
         for p in range(2):
             waiting[p].wait_recv()
             for d in range(1, 4):
-                push(spot_of(p, d), spot_of(p, d), sems(p, 5), peer(core=1))
-            waiting[p] = group(ar_out.at[n, p, :1024], sems(p, 5))
+                push(spot_of(p, d), spot_of(p, d), sems(p, 3), peer(core=1))
+            waiting[p] = group(ar_out.at[p, :, :1024], sems(p, 3))
         yield
         for p in range(2):
             waiting[p].wait_recv()
-            first = (1 - n) * HALF + p * 128
-            for i in range(3):
-                w_outs[i][:, first : first + 128] = ar_out[n, p, i * 512 : (i + 1) * 512]
-            for i in range(2):
-                low, column = (1 - n) * HALF, i * HALF + p * 128
-                w_outs[3][low : low + HALF, column : column + 128] = ar_out[
-                    n, p, 1536 + i * HALF : 1536 + (i + 1) * HALF
-                ]
+            for n in range(2):
+                low = (1 - n) * HALF
+                first = low + p * 128
+                for i in range(3):
+                    w_outs[i][:, first : first + 128] = ar_out[p, n, i * 512 : (i + 1) * 512]
+                for i in range(2):
+                    column = i * HALF + p * 128
+                    w_outs[3][low : low + HALF, column : column + 128] = ar_out[
+                        p, n, 1536 + i * HALF : 1536 + (i + 1) * HALF
+                    ]
         yield
 
     back_copy.wait_recv()
@@ -426,41 +435,36 @@
 
     lax.fori_loop(0, elecs, end_time, 0)
     weight_rows(acc_in_t, acc_out_t, ar_src.at[0])
-    time_sum, space_sum = summing(0), summing(1)
+    time_sum, space_sum, both = gather(0), gather(1), finish()
     next(time_sum)
     spatial_project(0)
-    next(time_sum)
+    send_raw(2)
     spatial_attend(0)
     next(time_sum)
-    send_raw(2)
     spatial_end(0)
     spatial_project(1)
-    next(time_sum)
-    send_back(0, (2,))
-    send_back(0, (1, 3))
     spatial_attend(1)
     spatial_end(1)
     spatial_project(2)
-    next(time_sum)
+    send_back(0, (2,))
+    send_back(0, (1, 3))
     spatial_attend(2)
     spatial_end(2)
     weight_rows(acc_in_s, acc_out_s, ar_src.at[1])
     next(space_sum)
-    next(time_sum)
     next(space_sum)
-    next(time_sum)
-    next(space_sum)
-    send_back(1, (1, 3))
-    place(0)
-    next(space_sum)
-    send_back(1, (2,))
     send_back(2, (2,))
     send_back(2, (1, 3))
-    next(space_sum)
-    next(space_sum)
+    next(both)
+    place(0)
+    next(both)
+    send_back(1, (2,))
+    send_back(1, (1, 3))
+    place(2)
+    next(both)
+    next(both)
     place(1)
-    place(2)
-    next(space_sum)
+    next(both)
     for whole in pending:
         whole.wait_send()
 
@@ -499,13 +503,14 @@
         + [vm((width, 3 * HALF), F32), vm((HALF, width), F32)] * 2
         + [vm((2, 2, 2048, 128), BF16)]
         + [vm((2, 2, 1024, 128), BF16)] * 2
-        + [vm((2, 2, 3, 256, 128), BF16), vm((2, 2, 256, 128), BF16), vm((2, 2, 15, 16, 128), BF16)]
+        + [vm((2, 2, 3, 256, 128), BF16), vm((2, 2, 256, 128), BF16), vm((2, 15, 2, 16, 128), BF16)]
         + [vm((2, 2, 2048, 128), BF16)]
         + [vm((WIN, HEADS * WIN), t) for t in (F32, BF16, BF16, F32)]
         + [dma((11,)), dma((2,)), dma((2,))]
         + [dma((3, 2))] * 2
         + [dma((3, 2))] * 2
-        + [dma((2, 2, 6))] * 2
+        + [dma((2, 2, 2))] * 2
+        + [dma((2, 4))] * 2
     )
     grad_inputs, *grads = pl.pallas_call(
         layer_kernel,

time: 93 us -> 87.8 us (0.944)
  Pallas kernels: 92.2 us -> 87.1 us
    pallas_call x1, Pallas kernels: 87.5 us -> 82.4 us  [shards(): pl.pallas_call(layer_kernel, out_shape=(sds(tokens + (width,), BF16),) +...]
where the time goes in v7:
time: 87.8 us; the launch traced here: 87.7 us
  Pallas kernels  87.1 us (99%)
    pallas_call x1, Pallas kernels, shards(): pl.pallas_call(layer_kernel, out_shape=(sds(tokens + (width,), BF16),) +...  82.4 us
    pallas_call x1, Pallas kernels, shards(): pl.pallas_call(end_kernel, out_shape=(sds(tokens + (width,), BF16),) + (s...  4.7 us

profile of v7, /device:TPU:1, one launch (start us, length us, event | category | flops | bytes accessed | tf_op | source)
XLA Modules:
  0.0 87.7 jit_solution(368141417222320438)
XLA Ops:
  0.6 82.4 %shard_map.101 = (bf16[4,384,512]{2,1,0:T(8,128)(2,1)}, bf16[512,512]{1,0:T(8,128)(2,1)}, bf16[512,512]{1,0:T(8,128)(2,1)}, bf16[512,512]{1,0:T(8,128)(2,1)}, bf16[512,512]{1,0:T(8,128)(2,1)}) custom-call(bf16[4,384,512]{2,1,0:T(8,128)(2,1)} %bitcast.3, bf16[4,384,512]{2,1,0:T(8,128)(2,1)} %bitcast.4, bf16[512,512]{1,0:T(8,128)(2,1)} %wq_h.1, ...), custom_call_target="tpu_custom_call" | custom-call | flops 20000000000 | bytes 10000000 | tf_op jit(solution)/shard_map/pallas_call | solution.py:515
  83.0 4.7 %shard_map.102 = (bf16[4,384,512]{2,1,0:T(8,128)(2,1)}, f32[512,512]{1,0:T(8,128)}, f32[512,512]{1,0:T(8,128)}, f32[512,512]{1,0:T(8,128)}, f32[512,512]{1,0:T(8,128)}) custom-call(bf16[4,384,512]{2,1,0:T(8,128)(2,1)} %get-tuple-element.15.dx, bf16[512,512]{1,0:T(8,128)(2,1)} %get-tuple-element.16.g0, bf16[512,512]{1,0:T(8,128)(2,1)} %get-tuple-element.17.g1, ...), custom_call_target="tpu_custom_call" | custom-call | tf_op jit(solution)/shard_map/pallas_call | solution.py:526

commit v8 on v6

--- a/solution.py
+++ b/solution.py
@@ -429,19 +429,18 @@
     time_sum, space_sum = summing(0), summing(1)
     next(time_sum)
     spatial_project(0)
-    next(time_sum)
+    send_raw(2)
     spatial_attend(0)
     next(time_sum)
-    send_raw(2)
     spatial_end(0)
     spatial_project(1)
     next(time_sum)
-    send_back(0, (2,))
-    send_back(0, (1, 3))
     spatial_attend(1)
     spatial_end(1)
     spatial_project(2)
     next(time_sum)
+    send_back(0, (2,))
+    send_back(0, (1, 3))
     spatial_attend(2)
     spatial_end(2)
     weight_rows(acc_in_s, acc_out_s, ar_src.at[1])
@@ -450,13 +449,14 @@
     next(space_sum)
     next(time_sum)
     next(space_sum)
+    next(space_sum)
+    send_back(1, (2,))
     send_back(1, (1, 3))
-    place(0)
-    next(space_sum)
-    send_back(1, (2,))
     send_back(2, (2,))
     send_back(2, (1, 3))
-    next(space_sum)
+    place(0)
+    next(space_sum)
+    next(time_sum)
     next(space_sum)
     place(1)
     place(2)

time: 93 us -> 88 us (0.946)
  Pallas kernels: 92.2 us -> 87.3 us
    pallas_call x1, Pallas kernels: 87.5 us -> 82.6 us  [shards(): pl.pallas_call(layer_kernel, out_shape=(sds(tokens + (width,), BF16),) +...]
where the time goes in v8:
time: 88 us; the launch traced here: 87.9 us
  Pallas kernels  87.3 us (99%)
    pallas_call x1, Pallas kernels, shards(): pl.pallas_call(layer_kernel, out_shape=(sds(tokens + (width,), BF16),) +...  82.6 us
    pallas_call x1, Pallas kernels, shards(): pl.pallas_call(end_kernel, out_shape=(sds(tokens + (width,), BF16),) + (s...  4.7 us

profile of v8, /device:TPU:1, one launch (start us, length us, event | category | flops | bytes accessed | tf_op | source)
XLA Modules:
  0.0 87.9 jit_solution(16801027508600862225)
XLA Ops:
  0.6 82.6 %shard_map.101 = (bf16[4,384,512]{2,1,0:T(8,128)(2,1)}, bf16[512,512]{1,0:T(8,128)(2,1)}, bf16[512,512]{1,0:T(8,128)(2,1)}, bf16[512,512]{1,0:T(8,128)(2,1)}, bf16[512,512]{1,0:T(8,128)(2,1)}) custom-call(bf16[4,384,512]{2,1,0:T(8,128)(2,1)} %bitcast.3, bf16[4,384,512]{2,1,0:T(8,128)(2,1)} %bitcast.4, bf16[512,512]{1,0:T(8,128)(2,1)} %wq_h.1, ...), custom_call_target="tpu_custom_call" | custom-call | flops 20000000000 | bytes 10000000 | tf_op jit(solution)/shard_map/pallas_call | solution.py:510
  83.2 4.7 %shard_map.102 = (bf16[4,384,512]{2,1,0:T(8,128)(2,1)}, f32[512,512]{1,0:T(8,128)}, f32[512,512]{1,0:T(8,128)}, f32[512,512]{1,0:T(8,128)}, f32[512,512]{1,0:T(8,128)}) custom-call(bf16[4,384,512]{2,1,0:T(8,128)(2,1)} %get-tuple-element.15.dx, bf16[512,512]{1,0:T(8,128)(2,1)} %get-tuple-element.16.g0, bf16[512,512]{1,0:T(8,128)(2,1)} %get-tuple-element.17.g1, ...), custom_call_target="tpu_custom_call" | custom-call | tf_op jit(solution)/shard_map/pallas_call | solution.py:521

commit v9 on v3

--- a/solution.py
+++ b/solution.py
@@ -65,7 +65,13 @@
         apart[:, at] = far
 
 
-def temporal_block(q, ga, k, v, bias, older, older_low, newer_low):
+def diagonal(cols):
+    return jnp.concatenate(
+        [cols[h * HEAD : (h + 1) * HEAD, h * WIN : (h + 1) * WIN] for h in range(HEADS)], axis=0
+    )
+
+
+def temporal_block(q, ga, k, v, k_cols, v_cols, bias, older, older_low, newer_low):
     qs, gs = stack_heads(q), stack_heads(ga)
     st = mm(k, qs, NT)
     gt = mm(v, gs, NT)
@@ -74,9 +80,9 @@
     probs, grad = soft(jnp.where(old, early, st[WIN:]), jnp.where(old, gt[:WIN], gt[WIN:]))
     pt = jnp.concatenate([probs * older_low[...], probs * newer_low[...]], axis=0)
     dt = jnp.concatenate([grad * older_low[...], grad * newer_low[...]], axis=0)
-    att = pick_heads(mm(pt, v, TN))
-    dq = pick_heads(mm(dt, k, TN)) * SCALE
-    return att, dq, mm(dt, qs, NN), mm(pt, gs, NN)
+    att = diagonal(mm(v_cols, pt, NN)).astype(BF16)
+    dq = (diagonal(mm(k_cols, dt, NN)) * SCALE).astype(BF16)
+    return att, dq.T, mm(dt, qs, NN), mm(pt, gs, NN)
 
 
 def spatial_block(q, ga, k, v, apart):
@@ -115,7 +121,7 @@
 def layer_kernel(x_h, cot_h, wq_h, wk_h, wv_h, wo_h, out, *rest):
     w_outs = rest[:4]
     (
-        xv, cv, halo, w_t, w_s, wo, q_t, k_t, v_t, g_t, dk_t, dv_t, att_t, dq_t, back_out, back_in, dx_t,
+        xv, cv, halo, w_t, w_s, wo, q_t, k_t, v_t, g_t, dk_t, dv_t, att_t, dq_t, kc_t, vc_t, back_out, back_in, dx_t,
         xr, cr, q_s, k_s, v_s, g_s, dxs, dxr, acc_in_t, acc_out_t, acc_in_s, acc_out_s,
         ar_src, recv_a, part, recv_b, ar_out, older, older_low, newer_low, apart,
         load_sem, halo_send, halo_recv, go_send, go_recv, ret_send, ret_recv, ar_send, ar_recv,
@@ -138,30 +144,6 @@
         low = 2 if axes[1] == "core" else 4
         return [(i, {axes[0]: i // low, axes[1]: i % low}) for i in range(1, 4 * low)]
 
-    near = {tuple(sorted(by.items())) for axes in (orders[0] + orders[1]) for _, by in others(axes)}
-    near = sorted({tuple((n, v) for n, v in by if v) for by in near})
-    barrier = pltpu.get_barrier_semaphore()
-    for device in [right, left] + [peer(**dict(by)) for by in near]:
-        pl.semaphore_signal(barrier, inc=1, device_id=device, device_id_type=MESH)
-    pl.semaphore_wait(barrier, 2 + len(near))
-
-    pending = []
-
-    def push(src, dst, sems, device):
-        pltpu.make_async_remote_copy(
-            src_ref=src, dst_ref=dst, send_sem=sems[0], recv_sem=sems[1], device_id=device, device_id_type=MESH
-        ).start()
-
-    def group(ref, sems):
-        whole = pltpu.make_async_remote_copy(
-            src_ref=ref, dst_ref=ref, send_sem=sems[0], recv_sem=sems[1], device_id=right, device_id_type=MESH
-        )
-        pending.append(whole)
-        return whole
-
-    def rows_at(first, size):
-        return pl.ds(pl.multiple_of(first, 16), size)
-
     loads = []
 
     def load(src, dst):
@@ -176,9 +158,33 @@
         load(w.at[:, HALF:], w_t.at[:, i * HALF : (i + 1) * HALF])
     for i, w in enumerate((wq_h, wk_h, wv_h)):
         load(w.at[:, :HALF], w_s.at[:, i * HALF : (i + 1) * HALF])
-    at = rows_at(y * quarter, quarter)
+    at = pl.ds(pl.multiple_of(y * quarter, 16), quarter)
     load(x_h.at[:, at], xr.at[:elecs])
     load(cot_h.at[:, at], cr.at[:elecs])
+    near = {tuple(sorted(by.items())) for axes in (orders[0] + orders[1]) for _, by in others(axes)}
+    near = sorted({tuple((n, v) for n, v in by if v) for by in near})
+    barrier = pltpu.get_barrier_semaphore()
+    for device in [right, left] + [peer(**dict(by)) for by in near]:
+        pl.semaphore_signal(barrier, inc=1, device_id=device, device_id_type=MESH)
+    pl.semaphore_wait(barrier, 2 + len(near))
+
+    pending = []
+
+    def push(src, dst, sems, device):
+        pltpu.make_async_remote_copy(
+            src_ref=src, dst_ref=dst, send_sem=sems[0], recv_sem=sems[1], device_id=device, device_id_type=MESH
+        ).start()
+
+    def group(ref, sems):
+        whole = pltpu.make_async_remote_copy(
+            src_ref=ref, dst_ref=ref, send_sem=sems[0], recv_sem=sems[1], device_id=right, device_id_type=MESH
+        )
+        pending.append(whole)
+        return whole
+
+    def rows_at(first, size):
+        return pl.ds(pl.multiple_of(first, 16), size)
+
     loads[0].wait()
     loads[1].wait()
     halo_sems = halo_send.at[0], halo_recv.at[0]
@@ -205,8 +211,10 @@
 
     def project_time(e, carry):
         q_t[e] = (mm(xv[e], w_t[:, :HALF], NN) * SCALE).astype(BF16)
-        k_t[e, WIN:] = mm(xv[e], w_t[:, HALF : 2 * HALF], NN).astype(BF16)
-        v_t[e, WIN:] = mm(xv[e], w_t[:, 2 * HALF :], NN).astype(BF16)
+        for own, cols, i in ((k_t, kc_t, 1), (v_t, vc_t, 2)):
+            t = mm(xv[e], w_t[:, i * HALF : (i + 1) * HALF], NN).astype(BF16)
+            own[e, WIN:] = t
+            cols[e, :, WIN:] = t.T
         g_t[e] = mm(cv[e], wo[HALF:, :], NT).astype(BF16)
         return carry
 
@@ -214,9 +222,11 @@
 
     def time_block(e, c, bias):
         rows, keys = slice(c * WIN, (c + 1) * WIN), slice(c * WIN, (c + 2) * WIN)
-        att, dq, dk, dv = temporal_block(q_t[e, rows], g_t[e, rows], k_t[e, keys], v_t[e, keys], bias, *masks)
-        att_t[e, rows] = att.astype(BF16)
-        dq_t[e, rows] = dq.astype(BF16)
+        att, dq, dk, dv = temporal_block(
+            q_t[e, rows], g_t[e, rows], k_t[e, keys], v_t[e, keys], kc_t[e, :, keys], vc_t[e, :, keys], bias, *masks
+        )
+        att_t[e, :, rows] = att
+        dq_t[e, rows] = dq
         return dk, dv
 
     def later_blocks(e, first_done):
@@ -231,8 +241,10 @@
             ref[e, 2 * WIN :] = two[WIN:]
 
     def first_block(e, first_done):
-        k_t[e, :WIN] = mm(halo[e], w_t[:, HALF : 2 * HALF], NN).astype(BF16)
-        v_t[e, :WIN] = mm(halo[e], w_t[:, 2 * HALF :], NN).astype(BF16)
+        for own, cols, i in ((k_t, kc_t, 1), (v_t, vc_t, 2)):
+            t = mm(halo[e], w_t[:, i * HALF : (i + 1) * HALF], NN).astype(BF16)
+            own[e, :WIN] = t
+            cols[e, :, :WIN] = t.T
         for side, (ref, grad) in enumerate(zip((dk_t, dv_t), time_block(e, 0, bias0))):
             back_out[side, e] = grad[:WIN].astype(BF16)
             if first_done:
@@ -401,7 +413,7 @@
         grads = jnp.concatenate([dq_t[e], full(dk_t, 0), full(dv_t, 1)], axis=1)
         dx_t[e] = mm(grads, w_t[...], NT)
         acc_in_t[...] += mm(xv[e], grads, TN)
-        acc_out_t[...] += mm(att_t[e], cv[e], TN)
+        acc_out_t[...] += mm(att_t[e], cv[e], NN)
         return carry
 
     lax.fori_loop(0, elecs, end_time, 0)
@@ -438,10 +450,22 @@
         whole.wait_send()
 
 
-def end_kernel(dx, g0, g1, g2, g3, out, o0, o1, o2, o3):
-    out[...] = dx[...]
-    for grad, o in zip((g0, g1, g2, g3), (o0, o1, o2, o3)):
-        o[...] = grad[...].astype(F32) * (1.0 / math.sqrt(196608))
+def end_kernel(*refs):
+    sources, outs = refs[:5], refs[5:10]
+    dx_v, grads_v, outs_v, in_sem, out_sem = refs[10:]
+    reads = [grads_v.at[i] for i in range(4)] + [dx_v]
+    writes = [outs_v.at[i] for i in range(4)] + [dx_v]
+    ins = [pltpu.make_async_copy(sources[i], reads[i], in_sem.at[i]) for i in range(5)]
+    for copy in ins:
+        copy.start()
+    back = [pltpu.make_async_copy(writes[i], outs[i], out_sem.at[i]) for i in range(5)]
+    for i in range(5):
+        ins[i].wait()
+        if i < 4:
+            outs_v[i] = grads_v[i].astype(F32) * (1.0 / math.sqrt(196608))
+        back[i].start()
+    for copy in back:
+        copy.wait()
 
 
 def sds(shape, dtype):
@@ -462,7 +486,8 @@
         + [vm((width, width), BF16)]
         + [vm(tokens + (HALF,), BF16), vm(ext + (HALF,), BF16), vm(ext + (HALF,), BF16), vm(tokens + (HALF,), BF16)]
         + [vm(tokens + (HALF,), F32)] * 2
-        + [vm(tokens + (HALF,), BF16)] * 2
+        + [vm((elecs, HALF, patches), BF16), vm(tokens + (HALF,), BF16)]
+        + [vm((elecs, HALF, patches + WIN), BF16)] * 2
         + [vm((2, elecs, WIN, HALF), BF16)] * 2
         + [vm(tokens + (width,), F32)]
         + [vm(everyone + (width,), BF16)] * 2
@@ -489,16 +514,21 @@
         ),
         cost_estimate=pl.CostEstimate(flops=2 * 10**10, bytes_accessed=10**7, transcendentals=2 * 10**6),
     )(inputs[0], cotangent[0], w_query, w_key, w_value, w_out)
-    token_spec = pl.BlockSpec((1, patches, width), lambda i: (i, 0, 0))
-    weight_spec = pl.BlockSpec((width // 4, width), lambda i: (i, 0))
-    grad_inputs, *grads = pl.pallas_call(
+    hbm = pl.BlockSpec(memory_space=pl.ANY)
+    *grads, grad_inputs = pl.pallas_call(
         end_kernel,
-        grid=(4,),
-        out_shape=(sds(tokens + (width,), BF16),) + (sds((width, width), F32),) * 4,
-        in_specs=[token_spec] + [weight_spec] * 4,
-        out_specs=(token_spec,) + (weight_spec,) * 4,
+        out_shape=(sds((width, width), F32),) * 4 + (sds(tokens + (width,), BF16),),
+        in_specs=[hbm] * 5,
+        out_specs=(hbm,) * 5,
+        scratch_shapes=[
+            vm(tokens + (width,), BF16),
+            vm((4, width, width), BF16),
+            vm((4, width, width), F32),
+            dma((5,)),
+            dma((5,)),
+        ],
         compiler_params=pltpu.CompilerParams(vmem_limit_bytes=VMEM_LIMIT),
-    )(grad_inputs, *grads)
+    )(*grads, grad_inputs)
     return (grad_inputs[None],) + tuple(grads)
 
 

time: 87.8 us -> 85 us (0.968)
  Pallas kernels: 86.9 us -> 84 us
    pallas_call x1, Pallas kernels: 81.9 us -> 80.3 us  [shards(): pl.pallas_call(layer_kernel, out_shape=(sds(tokens + (width,), BF16),) +...]
    pallas_call x1, Pallas kernels: 5.01 us -> 3.73 us  [shards(): pl.pallas_call(end_kernel, out_shape=(sds((width, width), F32),) * 4 + (s...]
where the time goes in v9:
time: 85 us; the launch traced here: 84.8 us
  Pallas kernels  84 us (99%)
    pallas_call x1, Pallas kernels, shards(): pl.pallas_call(layer_kernel, out_shape=(sds(tokens + (width,), BF16),) +...  80.3 us
    pallas_call x1, Pallas kernels, shards(): pl.pallas_call(end_kernel, out_shape=(sds((width, width), F32),) * 4 + (s...  3.73 us

profile of v9, /device:TPU:1, one launch (start us, length us, event | category | flops | bytes accessed | tf_op | source)
XLA Modules:
  0.0 84.8 jit_solution(14601515168144905540)
XLA Ops:
  0.6 80.3 %shard_map.101 = (bf16[4,384,512]{2,1,0:T(8,128)(2,1)}, bf16[512,512]{1,0:T(8,128)(2,1)}, bf16[512,512]{1,0:T(8,128)(2,1)}, bf16[512,512]{1,0:T(8,128)(2,1)}, bf16[512,512]{1,0:T(8,128)(2,1)}) custom-call(bf16[4,384,512]{2,1,0:T(8,128)(2,1)} %bitcast.3, bf16[4,384,512]{2,1,0:T(8,128)(2,1)} %bitcast.4, bf16[512,512]{1,0:T(8,128)(2,1)} %wq_h.1, ...), custom_call_target="tpu_custom_call" | custom-call | flops 20000000000 | bytes 10000000 | tf_op jit(solution)/shard_map/pallas_call | solution.py:506
  80.9 3.7 %shard_map.102 = (f32[512,512]{1,0:T(8,128)}, f32[512,512]{1,0:T(8,128)}, f32[512,512]{1,0:T(8,128)}, f32[512,512]{1,0:T(8,128)}, bf16[4,384,512]{2,1,0:T(8,128)(2,1)}) custom-call(bf16[512,512]{1,0:T(8,128)(2,1)} %get-tuple-element.15.refs_0_, bf16[512,512]{1,0:T(8,128)(2,1)} %get-tuple-element.16.refs_1_, bf16[512,512]{1,0:T(8,128)(2,1)} %get-tuple-element.17.refs_2_, ...), custom_call_target="tpu_custom_call" | custom-call | tf_op jit(solution)/shard_map/pallas_call | solution.py:518
